TPU v7x, 32 devices: a whole 2x2x4 slice. The times are simulated.
32 devices in a mesh: grp: 4 (over y, x), dap: 8 (over z, core).
Axes of the slice: x: 2, y: 2, z: 4, core: 2. Of those that a mesh axis runs over, the one named last changes fastest.
Arguments:
- pair_state: bfloat16 [8, 128, 128, 128], P('grp', 'dap'), may hold values from -6 to 6
- lengths: int32 [8], replicated, may hold values from 32 to 128, as said below
- norm_gain: float32 [3, 128], replicated, may hold values from 0.1 to 1.9
- norm_shift: float32 [3, 128], replicated, may hold values from -3 to 3
- attn_proj: bfloat16 [2, 128, 512], replicated
- bias_proj: bfloat16 [2, 128, 4], replicated, may hold values from -1.5 to 1.5
- attn_out: bfloat16 [2, 128, 128], replicated, may hold values from -0.5 to 0.5
- trans_up: bfloat16 [128, 512], replicated, may hold values from -0.5 to 0.5
- trans_down: bfloat16 [512, 128], replicated, may hold values from -0.25 to 0.25
Outputs:
- pair_out: bfloat16 [8, 128, 128, 128], P('grp', 'dap')
Inputs may be any that keep to these rules, and one draw needn't show every extreme that they name: `lengths`: residues of each protein; one protein has exactly 128.
All inputs are finite; a program needn't handle non-finite values.
Results may differ from a plain program's by a relative error of at most 0.035.
Values may be sent and summed in bfloat16 or wider, within the bound.
A program may use at most 128 MiB of HBM per device.

v0:
```python
from functools import partial

import jax
import jax.numpy as jnp
from jax import lax
from jax.sharding import PartitionSpec as P

HEADS = 4
HEAD_DIM = 32
KEY_BLOCK = 128
ROW_BLOCK = 4


EPSILON = 1e-05
MASKED = -1000000000.0


def layer_norm(values, gain_row, shift_row):
    values = values.astype(jnp.float32)
    center = values - jnp.mean(values, -1, keepdims=True)
    spread = jnp.mean(center * center, -1, keepdims=True)
    return (center * lax.rsqrt(spread + EPSILON) * gain_row + shift_row).astype(jnp.bfloat16)


def lookup(table, index):
    return jnp.sum(jnp.where(jnp.arange(table.shape[0], dtype=jnp.int32) == index, table, 0))


def attention_block(projected, bias_one, length):
    row_count, width_all, four_chans = projected.shape
    chans = four_chans // 4
    query = (
        (projected[..., :chans] * HEAD_DIM ** (-0.5))
        .astype(jnp.bfloat16)
        .reshape(row_count, width_all, HEADS, HEAD_DIM)
    )
    keyed = (
        projected[..., chans : 2 * chans]
        .astype(jnp.bfloat16)
        .reshape(row_count, width_all, HEADS, HEAD_DIM)
    )
    valued = (
        projected[..., 2 * chans : 3 * chans]
        .astype(jnp.bfloat16)
        .reshape(row_count, width_all, HEADS, HEAD_DIM)
    )
    key_blocks = (length + KEY_BLOCK - 1) // KEY_BLOCK

    def one_step(block_index, carry):
        running_top, running_total, accum = carry
        key_start = block_index * KEY_BLOCK
        key_part = lax.dynamic_slice_in_dim(keyed, key_start, KEY_BLOCK, 1)
        value_part = lax.dynamic_slice_in_dim(valued, key_start, KEY_BLOCK, 1)
        bias_part = lax.dynamic_slice_in_dim(bias_one, key_start, KEY_BLOCK, 2)
        scores = jnp.einsum("rjhd,rkhd->rhjk", query, key_part, preferred_element_type=jnp.float32)
        scores = scores + bias_part.astype(jnp.float32)[None]
        live = key_start + jnp.arange(KEY_BLOCK, dtype=jnp.int32) < length
        scores = jnp.where(live, scores, MASKED)
        new_top = jnp.maximum(running_top, jnp.max(scores, -1))
        fading = jnp.exp(running_top - new_top)
        weights = jnp.exp(scores - new_top[..., None])
        running_total = running_total * fading + jnp.sum(weights, -1)
        accum = accum * fading[..., None] + jnp.einsum(
            "rhjk,rkhd->rhjd",
            weights.astype(jnp.bfloat16),
            value_part,
            preferred_element_type=jnp.float32,
        )
        return (new_top, running_total, accum)

    start_top = jnp.full((row_count, HEADS, width_all), -jnp.inf, jnp.float32)
    start_total = jnp.zeros((row_count, HEADS, width_all), jnp.float32)
    start_accum = jnp.zeros((row_count, HEADS, width_all, HEAD_DIM), jnp.float32)
    final_top, final_total, final_accum = lax.fori_loop(
        0, key_blocks, one_step, (start_top, start_total, start_accum)
    )
    mixed = final_accum / final_total[..., None]
    mixed = jnp.transpose(mixed, (0, 2, 1, 3)).reshape(row_count, width_all, chans)
    return (mixed * jax.nn.sigmoid(projected[..., 3 * chans :])).astype(jnp.bfloat16)


def row_update(normed_one, bias_one, length, proj_in, proj_out, offset):
    width_all = normed_one.shape[1]
    chans = normed_one.shape[2]
    rows_in = lax.dynamic_slice_in_dim(normed_one, offset, ROW_BLOCK, 0)
    projected = jnp.dot(rows_in.reshape(-1, chans), proj_in, preferred_element_type=jnp.float32)
    gated = attention_block(projected.reshape(ROW_BLOCK, width_all, 4 * chans), bias_one, length)
    result = jnp.dot(gated.reshape(-1, chans), proj_out, preferred_element_type=jnp.float32)
    return result.reshape(ROW_BLOCK, width_all, chans)


def trans_update(normed_one, up_proj, down_proj, offset):
    width_all = normed_one.shape[1]
    chans = normed_one.shape[2]
    rows_in = lax.dynamic_slice_in_dim(normed_one, offset, ROW_BLOCK, 0)
    hidden_units = jax.nn.relu(
        jnp.dot(rows_in.reshape(-1, chans), up_proj, preferred_element_type=jnp.float32)
    ).astype(jnp.bfloat16)
    result = jnp.dot(hidden_units, down_proj, preferred_element_type=jnp.float32)
    return result.reshape(ROW_BLOCK, width_all, chans)


def masked_blocks(compute, length, first_row, rows_dev, width_all, chans):
    col_live = jnp.arange(width_all, dtype=jnp.int32) < length

    def one_block(start):

        def work(offset):
            row_live = first_row + offset + jnp.arange(ROW_BLOCK, dtype=jnp.int32) < length
            cells = row_live[:, None, None] & col_live[None, :, None]
            return jnp.where(cells, compute(offset), 0.0)

        def skipped(offset):
            return jnp.zeros((ROW_BLOCK, width_all, chans), jnp.float32)

        return lax.cond(first_row + start < length, work, skipped, start)

    starts = jnp.arange(0, rows_dev, ROW_BLOCK, dtype=jnp.int32)
    return lax.map(one_block, starts).reshape(rows_dev, width_all, chans)


def attend(state, lens, first_row, gain_row, shift_row, proj_in, proj_bias, proj_out):
    per_group, rows_dev, width_all, chans = state.shape
    normed = layer_norm(state, gain_row, shift_row)
    bias_local = jnp.einsum(
        "prlc,ch->phrl", normed, proj_bias, preferred_element_type=jnp.float32
    ).astype(jnp.bfloat16)
    bias_all = lax.all_gather(bias_local, "dap", axis=2, tiled=True)
    updates = []
    for member in range(per_group):
        compute = partial(
            row_update, normed[member], bias_all[member], lens[member], proj_in, proj_out
        )
        updates.append(masked_blocks(compute, lens[member], first_row, rows_dev, width_all, chans))
    return (state.astype(jnp.float32) + jnp.stack(updates)).astype(jnp.bfloat16)


def transition(state, lens, first_row, gain_row, shift_row, up_proj, down_proj):
    per_group, rows_dev, width_all, chans = state.shape
    normed = layer_norm(state, gain_row, shift_row)
    updates = []
    for member in range(per_group):
        compute = partial(trans_update, normed[member], up_proj, down_proj)
        updates.append(masked_blocks(compute, lens[member], first_row, rows_dev, width_all, chans))
    return (state.astype(jnp.float32) + jnp.stack(updates)).astype(jnp.bfloat16)


def transpose_pair(state):
    arrived = lax.all_to_all(state, "dap", split_axis=2, concat_axis=1, tiled=True)
    return jnp.swapaxes(arrived, 1, 2)


def run_block(
    hosted, lens, norm_gain, norm_shift, attn_proj, bias_proj, attn_out, trans_up, trans_down
):
    first_row = lax.axis_index("dap") * hosted.shape[1]
    first = attend(
        hosted,
        lens,
        first_row,
        norm_gain[0],
        norm_shift[0],
        attn_proj[0],
        bias_proj[0],
        attn_out[0],
    )
    flipped = transpose_pair(first)
    second = attend(
        flipped,
        lens,
        first_row,
        norm_gain[1],
        norm_shift[1],
        attn_proj[1],
        bias_proj[1],
        attn_out[1],
    )
    third = transition(second, lens, first_row, norm_gain[2], norm_shift[2], trans_up, trans_down)
    return transpose_pair(third)


def on_device(
    pair_state, lengths, norm_gain, norm_shift, attn_proj, bias_proj, attn_out, trans_up, trans_down
):
    groups = lax.axis_size("grp")
    group = lax.axis_index("grp")
    per_group = pair_state.shape[0]
    table = lengths.reshape(groups, per_group)
    own_lens = lax.dynamic_index_in_dim(table, group, 0, keepdims=False)
    weights_all = (norm_gain, norm_shift, attn_proj, bias_proj, attn_out, trans_up, trans_down)
    group_ids = jnp.arange(groups, dtype=jnp.int32)
    order_first = jnp.argsort(-table[:, 0], stable=True)
    order_last = jnp.argsort(table[:, per_group - 1], stable=True)
    dest_of = jnp.sum(
        jnp.where(order_last[None, :] == group_ids[:, None], order_first[None, :], 0), 1
    )
    source_of = jnp.sum(
        jnp.where(order_first[None, :] == group_ids[:, None], order_last[None, :], 0), 1
    )
    mine_dest = lookup(dest_of, group)
    mine_source = lookup(source_of, group)
    guest_len = lookup(lengths, mine_source * per_group + per_group - 1)
    blank = jnp.zeros((groups,) + pair_state.shape[1:], jnp.bfloat16)
    outgoing = lax.dynamic_update_index_in_dim(blank, pair_state[per_group - 1], mine_dest, 0)
    arrived = lax.all_to_all(outgoing, "grp", split_axis=0, concat_axis=0, tiled=True)
    guest = lax.dynamic_index_in_dim(arrived, mine_source, 0, keepdims=True)
    hosted = jnp.concatenate([pair_state[: per_group - 1], guest], 0)
    hosted_lens = jnp.concatenate([own_lens[: per_group - 1], guest_len[None]], 0)
    result = run_block(hosted, hosted_lens, *weights_all)
    homeward = lax.dynamic_update_index_in_dim(blank, result[per_group - 1], mine_source, 0)
    returned = lax.all_to_all(homeward, "grp", split_axis=0, concat_axis=0, tiled=True)
    own_last = lax.dynamic_index_in_dim(returned, mine_dest, 0, keepdims=True)
    return jnp.concatenate([result[: per_group - 1], own_last], 0)


def solution(mesh):
    in_specs = (P("grp", "dap", None, None), P(), P(), P(), P(), P(), P(), P(), P())
    out_specs = P("grp", "dap", None, None)
    return jax.shard_map(
        on_device, mesh=mesh, in_specs=in_specs, out_specs=out_specs, check_vma=False
    )
```

profile of v0, /device:TPU:0, one launch (start us, length us, event | category | flops | bytes accessed | tf_op | source)
XLA Modules:
  0.0 531.1 jit_solution(12811476667091545304)
XLA Ops:
  6.4 1.6 broadcast_in_dim.190.clone
  9.2 5.3 all-to-all-start
  21.7 18.6 %all-to-all-done = bf16[4,16,128,128]{3,1,2,0:T(8,128)(2,1)} async-done(((bf16[4,16,128,128]{3,1,2,0:T(8,128)(2,1)}), bf16[4,16,128,128]{3,1,2,0:T(8,128)(2,1)}, u32[]{:S(2)}, u32[]{:S(2)}) %all-to-all-start) | async-done | bytes 2097184 | tf_op jit(solution)/shard_map/all_to_all | solution.py:205
  46.1 2.5 fusion.111
  48.9 14.6 %all_gather.6 = bf16[2,4,128,128]{3,1,0,2:T(4,128)(2,1)S(1)} all-gather(bf16[2,4,16,128]{3,1,0,2:T(4,128)(2,1)S(1)} %copy.331), channel_id=1, replica_groups=mesh['grp'=4,'dap'=8] {'dap'}, dimensions={2}, use_global_device_ids=true | all-gather | bytes 294912 | tf_op jit(solution)/shard_map/all_gather | solution.py:128
  65.5 48.8 %while.130 = (s32[]{:T(128)}, f32[4,4,128,128]{3,1,0,2:T(4,128)}, s32[4]{0:T(128)}, s32[]{:T(128)}, s32[]{:T(128)}, /*index=5*/bf16[16,128,128]{2,1,0:T(8,128)(2...) while((s32[]{:T(128)}, f32[4,4,128,128]{3,1,0,2:T(4,128)}, ...), condition=%wide.region_15.16_spmd.clone.clone, body=%wide.region_8.15_spmd.clone.clone.sunk | while | flops 120329120 | bytes 11071168 | solution.py:119
  68.5 8.3 %conditional.24 = (f32[1,4,128,128]{3,2,1,0:T(8,128)S(1)}) conditional(s32[]{:T(128)} %convert_element_type.275, () %tuple.346, (s32[]{:T(128)}, s32[]{:T(128)}, s32[]{:T(128)}, s32[128]{0:T(128)}, bf16[16,128,128]{2,1,0:T(8,128)(2,1)S(1)}, /*index=5*/bf16[128,512]{1,0:T(8,128)(2,1)S(1)}, bf16[4,128,128]{1,2,0:T(8,128)(2,1)S(1)}, ...), branch_computations={%region_9.9_spmd, %region_10.14_spmd} | conditional | flops 120329112 | bytes 10545645 | solution.py:116
  80.7 8.3 %conditional.24 = (f32[1,4,128,128]{3,2,1,0:T(8,128)S(1)}) conditional(s32[]{:T(128)} %convert_element_type.275, () %tuple.346, (s32[]{:T(128)}, s32[]{:T(128)}, s32[]{:T(128)}, s32[128]{0:T(128)}, bf16[16,128,128]{2,1,0:T(8,128)(2,1)S(1)}, /*index=5*/bf16[128,512]{1,0:T(8,128)(2,1)S(1)}, bf16[4,128,128]{1,2,0:T(8,128)(2,1)S(1)}, ...), branch_computations={%region_9.9_spmd, %region_10.14_spmd} | conditional | flops 120329112 | bytes 10545645 | solution.py:116
  92.9 8.3 %conditional.24 = (f32[1,4,128,128]{3,2,1,0:T(8,128)S(1)}) conditional(s32[]{:T(128)} %convert_element_type.275, () %tuple.346, (s32[]{:T(128)}, s32[]{:T(128)}, s32[]{:T(128)}, s32[128]{0:T(128)}, bf16[16,128,128]{2,1,0:T(8,128)(2,1)S(1)}, /*index=5*/bf16[128,512]{1,0:T(8,128)(2,1)S(1)}, bf16[4,128,128]{1,2,0:T(8,128)(2,1)S(1)}, ...), branch_computations={%region_9.9_spmd, %region_10.14_spmd} | conditional | flops 120329112 | bytes 10545645 | solution.py:116
  105.1 8.3 %conditional.24 = (f32[1,4,128,128]{3,2,1,0:T(8,128)S(1)}) conditional(s32[]{:T(128)} %convert_element_type.275, () %tuple.346, (s32[]{:T(128)}, s32[]{:T(128)}, s32[]{:T(128)}, s32[128]{0:T(128)}, bf16[16,128,128]{2,1,0:T(8,128)(2,1)S(1)}, /*index=5*/bf16[128,512]{1,0:T(8,128)(2,1)S(1)}, bf16[4,128,128]{1,2,0:T(8,128)(2,1)S(1)}, ...), branch_computations={%region_9.9_spmd, %region_10.14_spmd} | conditional | flops 120329112 | bytes 10545645 | solution.py:116
  117.7 52.8 %while.131 = (s32[]{:T(128)}, f32[4,4,128,128]{3,1,0,2:T(4,128)}, s32[4]{0:T(128)}, s32[]{:T(128)}, s32[]{:T(128)}, /*index=5*/bf16[16,128,128]{2,1,0:T(8,128)(2...) while((s32[]{:T(128)}, f32[4,4,128,128]{3,1,0,2:T(4,128)}, ...), condition=%wide.region_24.25_spmd.clone.clone, body=%wide.region_17.24_spmd.clone.clone.sunk | while | flops 120329120 | bytes 11071168 | solution.py:119
  120.9 9.1 %conditional.25 = (f32[1,4,128,128]{3,2,1,0:T(8,128)S(1)}) conditional(s32[]{:T(128)} %convert_element_type.276, () %tuple.349, (s32[]{:T(128)}, s32[]{:T(128)}, s32[]{:T(128)}, s32[128]{0:T(128)}, bf16[16,128,128]{2,1,0:T(8,128)(2,1)S(1)}, /*index=5*/bf16[128,512]{1,0:T(8,128)(2,1)S(1)}, bf16[4,128,128]{1,2,0:T(8,128)(2,1)S(1)}, ...), branch_computations={%region_18.18_spmd, %region_19.23_spmd} | conditional | flops 120329112 | bytes 10545645 | solution.py:116
  124.5 1.6 while.127
  134.1 9.1 %conditional.25 = (f32[1,4,128,128]{3,2,1,0:T(8,128)S(1)}) conditional(s32[]{:T(128)} %convert_element_type.276, () %tuple.349, (s32[]{:T(128)}, s32[]{:T(128)}, s32[]{:T(128)}, s32[128]{0:T(128)}, bf16[16,128,128]{2,1,0:T(8,128)(2,1)S(1)}, /*index=5*/bf16[128,512]{1,0:T(8,128)(2,1)S(1)}, bf16[4,128,128]{1,2,0:T(8,128)(2,1)S(1)}, ...), branch_computations={%region_18.18_spmd, %region_19.23_spmd} | conditional | flops 120329112 | bytes 10545645 | solution.py:116
  137.7 1.6 while.127
  147.3 9.1 %conditional.25 = (f32[1,4,128,128]{3,2,1,0:T(8,128)S(1)}) conditional(s32[]{:T(128)} %convert_element_type.276, () %tuple.349, (s32[]{:T(128)}, s32[]{:T(128)}, s32[]{:T(128)}, s32[128]{0:T(128)}, bf16[16,128,128]{2,1,0:T(8,128)(2,1)S(1)}, /*index=5*/bf16[128,512]{1,0:T(8,128)(2,1)S(1)}, bf16[4,128,128]{1,2,0:T(8,128)(2,1)S(1)}, ...), branch_computations={%region_18.18_spmd, %region_19.23_spmd} | conditional | flops 120329112 | bytes 10545645 | solution.py:116
  150.9 1.6 while.127
  160.5 9.1 %conditional.25 = (f32[1,4,128,128]{3,2,1,0:T(8,128)S(1)}) conditional(s32[]{:T(128)} %convert_element_type.276, () %tuple.349, (s32[]{:T(128)}, s32[]{:T(128)}, s32[]{:T(128)}, s32[128]{0:T(128)}, bf16[16,128,128]{2,1,0:T(8,128)(2,1)S(1)}, /*index=5*/bf16[128,512]{1,0:T(8,128)(2,1)S(1)}, bf16[4,128,128]{1,2,0:T(8,128)(2,1)S(1)}, ...), branch_computations={%region_18.18_spmd, %region_19.23_spmd} | conditional | flops 120329112 | bytes 10545645 | solution.py:116
  164.1 1.6 while.127
  170.5 1.9 fusion.108
  173.5 3.7 all-to-all-start.1
  177.2 26.3 %all-to-all-done.1 = bf16[2,16,128,128]{3,1,0,2:T(8,128)(2,1)S(1)} async-done(((bf16[2,16,128,128]{3,1,0,2:T(8,128)(2,1)}), bf16[2,16,128,128]{3,1,0,2:T(8,128)(2,1)S(1)}, u32[]{:S(2)}, u32[]{:S(2)}) %all-to-all-start.1) | async-done | bytes 1048608 | tf_op jit(solution)/shard_map/all_to_all | solution.py:149
  210.1 2.5 fusion.112
  213.8 14.2 %all_gather.7 = bf16[2,4,128,128]{3,1,0,2:T(4,128)(2,1)S(1)} all-gather(bf16[2,4,16,128]{3,1,0,2:T(4,128)(2,1)S(1)} %copy.345), channel_id=1, replica_groups=mesh['grp'=4,'dap'=8] {'dap'}, dimensions={2}, use_global_device_ids=true | all-gather | bytes 294912 | tf_op jit(solution)/shard_map/all_gather | solution.py:128
  230.0 62.7 %while.132 = (s32[]{:T(128)}, f32[4,4,128,128]{3,1,0,2:T(4,128)}, s32[4]{0:T(128)}, s32[]{:T(128)}, s32[]{:T(128)}, /*index=5*/bf16[16,128,128]{2,1,0:T(8,128)(2...) while((s32[]{:T(128)}, f32[4,4,128,128]{3,1,0,2:T(4,128)}, ...), condition=%wide.region_34.35_spmd.clone.clone, body=%wide.region_27.34_spmd.clone.clone.sunk | while | flops 120329120 | bytes 15396600 | solution.py:119
  232.5 12.3 %conditional.26 = (f32[1,4,128,128]{3,2,1,0:T(8,128)S(1)}) conditional(s32[]{:T(128)} %convert_element_type.277, () %tuple.352, (s32[]{:T(128)}, s32[]{:T(128)}, s32[]{:T(128)}, s32[128]{0:T(128)S(1)}, bf16[16,128,128]{2,1,0:T(8,128)(2,1)}, /*index=5*/bf16[128,512]{1,0:T(8,128)(2,1)}, bf16[4,128,128]{1,2,0:T(8,128)(2,1)S(1)}, ...), branch_computations={%region_28.28_spmd, %region_29.33_spmd} | conditional | flops 120329112 | bytes 14871077 | solution.py:116
  248.1 12.3 %conditional.26 = (f32[1,4,128,128]{3,2,1,0:T(8,128)S(1)}) conditional(s32[]{:T(128)} %convert_element_type.277, () %tuple.352, (s32[]{:T(128)}, s32[]{:T(128)}, s32[]{:T(128)}, s32[128]{0:T(128)S(1)}, bf16[16,128,128]{2,1,0:T(8,128)(2,1)}, /*index=5*/bf16[128,512]{1,0:T(8,128)(2,1)}, bf16[4,128,128]{1,2,0:T(8,128)(2,1)S(1)}, ...), branch_computations={%region_28.28_spmd, %region_29.33_spmd} | conditional | flops 120329112 | bytes 14871077 | solution.py:116
  263.8 12.3 %conditional.26 = (f32[1,4,128,128]{3,2,1,0:T(8,128)S(1)}) conditional(s32[]{:T(128)} %convert_element_type.277, () %tuple.352, (s32[]{:T(128)}, s32[]{:T(128)}, s32[]{:T(128)}, s32[128]{0:T(128)S(1)}, bf16[16,128,128]{2,1,0:T(8,128)(2,1)}, /*index=5*/bf16[128,512]{1,0:T(8,128)(2,1)}, bf16[4,128,128]{1,2,0:T(8,128)(2,1)S(1)}, ...), branch_computations={%region_28.28_spmd, %region_29.33_spmd} | conditional | flops 120329112 | bytes 14871077 | solution.py:116
  279.5 12.3 %conditional.26 = (f32[1,4,128,128]{3,2,1,0:T(8,128)S(1)}) conditional(s32[]{:T(128)} %convert_element_type.277, () %tuple.352, (s32[]{:T(128)}, s32[]{:T(128)}, s32[]{:T(128)}, s32[128]{0:T(128)S(1)}, bf16[16,128,128]{2,1,0:T(8,128)(2,1)}, /*index=5*/bf16[128,512]{1,0:T(8,128)(2,1)}, bf16[4,128,128]{1,2,0:T(8,128)(2,1)S(1)}, ...), branch_computations={%region_28.28_spmd, %region_29.33_spmd} | conditional | flops 120329112 | bytes 14871077 | solution.py:116
  292.6 2.0 copy.349
  296.8 65.2 %while.133 = (s32[]{:T(128)}, f32[4,4,128,128]{3,1,0,2:T(4,128)}, s32[4]{0:T(128)}, s32[]{:T(128)}, s32[]{:T(128)}, /*index=5*/bf16[16,128,128]{2,1,0:T(8,128)(2...) while((s32[]{:T(128)}, f32[4,4,128,128]{3,1,0,2:T(4,128)}, ...), condition=%wide.region_42.43_spmd.clone.clone, body=%wide.region_35.42_spmd.clone.clone.sunk | while | flops 120329120 | bytes 15396600 | solution.py:119
  299.4 12.8 %conditional.27 = (f32[1,4,128,128]{3,2,1,0:T(8,128)S(1)}) conditional(s32[]{:T(128)} %convert_element_type.278, () %tuple.355, (s32[]{:T(128)}, s32[]{:T(128)}, s32[]{:T(128)}, s32[128]{0:T(128)S(1)}, bf16[16,128,128]{2,1,0:T(8,128)(2,1)}, /*index=5*/bf16[128,512]{1,0:T(8,128)(2,1)}, bf16[4,128,128]{1,2,0:T(8,128)(2,1)S(1)}, ...), branch_computations={%region_36.36_spmd, %region_37.41_spmd} | conditional | flops 120329112 | bytes 14871077 | solution.py:116
  307.1 1.6 while.129
  315.7 12.8 %conditional.27 = (f32[1,4,128,128]{3,2,1,0:T(8,128)S(1)}) conditional(s32[]{:T(128)} %convert_element_type.278, () %tuple.355, (s32[]{:T(128)}, s32[]{:T(128)}, s32[]{:T(128)}, s32[128]{0:T(128)S(1)}, bf16[16,128,128]{2,1,0:T(8,128)(2,1)}, /*index=5*/bf16[128,512]{1,0:T(8,128)(2,1)}, bf16[4,128,128]{1,2,0:T(8,128)(2,1)S(1)}, ...), branch_computations={%region_36.36_spmd, %region_37.41_spmd} | conditional | flops 120329112 | bytes 14871077 | solution.py:116
  323.5 1.6 while.129
  332.0 12.8 %conditional.27 = (f32[1,4,128,128]{3,2,1,0:T(8,128)S(1)}) conditional(s32[]{:T(128)} %convert_element_type.278, () %tuple.355, (s32[]{:T(128)}, s32[]{:T(128)}, s32[]{:T(128)}, s32[128]{0:T(128)S(1)}, bf16[16,128,128]{2,1,0:T(8,128)(2,1)}, /*index=5*/bf16[128,512]{1,0:T(8,128)(2,1)}, bf16[4,128,128]{1,2,0:T(8,128)(2,1)S(1)}, ...), branch_computations={%region_36.36_spmd, %region_37.41_spmd} | conditional | flops 120329112 | bytes 14871077 | solution.py:116
  339.7 1.6 while.129
  348.3 12.8 %conditional.27 = (f32[1,4,128,128]{3,2,1,0:T(8,128)S(1)}) conditional(s32[]{:T(128)} %convert_element_type.278, () %tuple.355, (s32[]{:T(128)}, s32[]{:T(128)}, s32[]{:T(128)}, s32[128]{0:T(128)S(1)}, bf16[16,128,128]{2,1,0:T(8,128)(2,1)}, /*index=5*/bf16[128,512]{1,0:T(8,128)(2,1)}, bf16[4,128,128]{1,2,0:T(8,128)(2,1)S(1)}, ...), branch_computations={%region_36.36_spmd, %region_37.41_spmd} | conditional | flops 120329112 | bytes 14871077 | solution.py:116
  356.0 1.6 while.129
  362.0 1.9 fusion.110
  365.9 2.4 fusion.100
  368.5 2.9 fusion.103
  374.5 45.4 %while.134 = (s32[]{:T(128)}, f32[4,4,128,128]{3,1,0,2:T(4,128)}, s32[4]{0:T(128)}, s32[]{:T(128)}, s32[]{:T(128)}, /*index=5*/bf16[16,128,128]{2,1,0:T(8,128)(2...) while((s32[]{:T(128)}, f32[4,4,128,128]{3,1,0,2:T(4,128)}, ...), condition=%wide.region_48.49_spmd.clone.clone, body=%wide.region_45.48_spmd.clone.clone.sunk | while | flops 134808192 | bytes 1969169 | solution.py:119
  377.0 7.9 %conditional.28 = (f32[1,4,128,128]{3,2,1,0:T(8,128)S(1)}) conditional(s32[]{:T(128)} %convert_element_type.279, () %tuple.358, (s32[]{:T(128)}, s32[]{:T(128)}, s32[]{:T(128)}, s32[128]{0:T(128)S(1)}, bf16[16,128,128]{2,1,0:T(8,128)(2,1)}, /*index=5*/bf16[128,512]{1,0:T(8,128)(2,1)S(1)}, bf16[512,128]{1,0:T(8,128)(2,1)}, s32[]{:T(128)}) %tuple.359), branch_computations={%region_46.46_spmd, %region_47.47_spmd} | conditional | flops 134808192 | bytes 1443662 | solution.py:116
  379.9 2.0 fusion.89
  388.3 7.9 %conditional.28 = (f32[1,4,128,128]{3,2,1,0:T(8,128)S(1)}) conditional(s32[]{:T(128)} %convert_element_type.279, () %tuple.358, (s32[]{:T(128)}, s32[]{:T(128)}, s32[]{:T(128)}, s32[128]{0:T(128)S(1)}, bf16[16,128,128]{2,1,0:T(8,128)(2,1)}, /*index=5*/bf16[128,512]{1,0:T(8,128)(2,1)S(1)}, bf16[512,128]{1,0:T(8,128)(2,1)}, s32[]{:T(128)}) %tuple.359), branch_computations={%region_46.46_spmd, %region_47.47_spmd} | conditional | flops 134808192 | bytes 1443662 | solution.py:116
  391.2 2.0 fusion.89
  399.6 7.9 %conditional.28 = (f32[1,4,128,128]{3,2,1,0:T(8,128)S(1)}) conditional(s32[]{:T(128)} %convert_element_type.279, () %tuple.358, (s32[]{:T(128)}, s32[]{:T(128)}, s32[]{:T(128)}, s32[128]{0:T(128)S(1)}, bf16[16,128,128]{2,1,0:T(8,128)(2,1)}, /*index=5*/bf16[128,512]{1,0:T(8,128)(2,1)S(1)}, bf16[512,128]{1,0:T(8,128)(2,1)}, s32[]{:T(128)}) %tuple.359), branch_computations={%region_46.46_spmd, %region_47.47_spmd} | conditional | flops 134808192 | bytes 1443662 | solution.py:116
  402.6 2.0 fusion.89
  411.0 7.9 %conditional.28 = (f32[1,4,128,128]{3,2,1,0:T(8,128)S(1)}) conditional(s32[]{:T(128)} %convert_element_type.279, () %tuple.358, (s32[]{:T(128)}, s32[]{:T(128)}, s32[]{:T(128)}, s32[128]{0:T(128)S(1)}, bf16[16,128,128]{2,1,0:T(8,128)(2,1)}, /*index=5*/bf16[128,512]{1,0:T(8,128)(2,1)S(1)}, bf16[512,128]{1,0:T(8,128)(2,1)}, s32[]{:T(128)}) %tuple.359), branch_computations={%region_46.46_spmd, %region_47.47_spmd} | conditional | flops 134808192 | bytes 1443662 | solution.py:116
  414.0 2.0 fusion.89
  419.8 2.0 copy.358
  422.9 46.8 %while.135 = (s32[]{:T(128)}, f32[4,4,128,128]{3,1,0,2:T(4,128)}, s32[4]{0:T(128)}, s32[]{:T(128)}, s32[]{:T(128)}, /*index=5*/bf16[16,128,128]{2,1,0:T(8,128)(2...) while((s32[]{:T(128)}, f32[4,4,128,128]{3,1,0,2:T(4,128)}, ...), condition=%wide.region_52.53_spmd.clone.clone, body=%wide.region_49.52_spmd.clone.clone.sunk | while | flops 134808192 | bytes 1969169 | solution.py:119
  425.5 8.2 %conditional.29 = (f32[1,4,128,128]{3,2,1,0:T(8,128)S(1)}) conditional(s32[]{:T(128)} %convert_element_type.280, () %tuple.361, (s32[]{:T(128)}, s32[]{:T(128)}, s32[]{:T(128)}, s32[128]{0:T(128)S(1)}, bf16[16,128,128]{2,1,0:T(8,128)(2,1)}, /*index=5*/bf16[128,512]{1,0:T(8,128)(2,1)S(1)}, bf16[512,128]{1,0:T(8,128)(2,1)}, s32[]{:T(128)}) %tuple.362), branch_computations={%region_50.50_spmd, %region_51.51_spmd} | conditional | flops 134808192 | bytes 1443662 | solution.py:116
  428.5 2.0 fusion.93
  437.3 8.2 %conditional.29 = (f32[1,4,128,128]{3,2,1,0:T(8,128)S(1)}) conditional(s32[]{:T(128)} %convert_element_type.280, () %tuple.361, (s32[]{:T(128)}, s32[]{:T(128)}, s32[]{:T(128)}, s32[128]{0:T(128)S(1)}, bf16[16,128,128]{2,1,0:T(8,128)(2,1)}, /*index=5*/bf16[128,512]{1,0:T(8,128)(2,1)S(1)}, bf16[512,128]{1,0:T(8,128)(2,1)}, s32[]{:T(128)}) %tuple.362), branch_computations={%region_50.50_spmd, %region_51.51_spmd} | conditional | flops 134808192 | bytes 1443662 | solution.py:116
  440.2 2.0 fusion.93
  449.0 8.2 %conditional.29 = (f32[1,4,128,128]{3,2,1,0:T(8,128)S(1)}) conditional(s32[]{:T(128)} %convert_element_type.280, () %tuple.361, (s32[]{:T(128)}, s32[]{:T(128)}, s32[]{:T(128)}, s32[128]{0:T(128)S(1)}, bf16[16,128,128]{2,1,0:T(8,128)(2,1)}, /*index=5*/bf16[128,512]{1,0:T(8,128)(2,1)S(1)}, bf16[512,128]{1,0:T(8,128)(2,1)}, s32[]{:T(128)}) %tuple.362), branch_computations={%region_50.50_spmd, %region_51.51_spmd} | conditional | flops 134808192 | bytes 1443662 | solution.py:116
  451.9 2.0 fusion.93
  460.7 8.2 %conditional.29 = (f32[1,4,128,128]{3,2,1,0:T(8,128)S(1)}) conditional(s32[]{:T(128)} %convert_element_type.280, () %tuple.361, (s32[]{:T(128)}, s32[]{:T(128)}, s32[]{:T(128)}, s32[128]{0:T(128)S(1)}, bf16[16,128,128]{2,1,0:T(8,128)(2,1)}, /*index=5*/bf16[128,512]{1,0:T(8,128)(2,1)S(1)}, bf16[512,128]{1,0:T(8,128)(2,1)}, s32[]{:T(128)}) %tuple.362), branch_computations={%region_50.50_spmd, %region_51.51_spmd} | conditional | flops 134808192 | bytes 1443662 | solution.py:116
  463.6 2.0 fusion.93
  469.8 2.3 fusion.109
  472.0 29.0 %all_to_all.37 = bf16[2,16,128,128]{3,1,0,2:T(8,128)(2,1)S(1)} all-to-all(bf16[2,16,128,128]{3,1,0,2:T(8,128)(2,1)S(1)} %fusion.109), channel_id=1, replica_groups=mesh['grp'=4,'dap'=8] {'dap'}, dimensions={2} | all-to-all | bytes 2097152 | tf_op jit(solution)/shard_map/all_to_all | solution.py:149
  502.0 27.8 %all_to_all.38 = bf16[4,16,128,128]{3,1,2,0:T(8,128)(2,1)S(1)} all-to-all(bf16[4,16,128,128]{3,1,2,0:T(8,128)(2,1)S(1)} %get-tuple-element.1676), channel_id=1, replica_groups=mesh['grp'=4,'dap'=8] {'grp'}, dimensions={0} | all-to-all | bytes 4194304 | tf_op jit(solution)/shard_map/all_to_all | solution.py:211
  (622 shorter events, 251.6 us)
Async XLA Ops:
  9.2 9.9 %copy-start.14 = (s32[8]{0:T(128)S(1)}, s32[8]{0:T(128)}, u32[]{:S(2)}) copy-start(s32[8]{0:T(128)} %param.42) | copy-start | bytes 100
  9.2 10.6 %copy-start.12 = (f32[3,128]{1,0:T(4,128)S(1)}, f32[3,128]{1,0:T(4,128)}, u32[]{:S(2)}) copy-start(f32[3,128]{1,0:T(4,128)} %param.44) | copy-start | bytes 4612
  9.2 10.6 %copy-start.13 = (f32[3,128]{1,0:T(4,128)S(1)}, f32[3,128]{1,0:T(4,128)}, u32[]{:S(2)}) copy-start(f32[3,128]{1,0:T(4,128)} %param.43) | copy-start | bytes 4612
  9.2 11.2 %copy-start.5 = (bf16[2,128,128]{2,1,0:T(8,128)(2,1)S(1)}, bf16[2,128,128]{2,1,0:T(8,128)(2,1)}, u32[]{:S(2)}) copy-start(bf16[2,128,128]{2,1,0:T(8,128)(2,1)} %param.47) | copy-start | bytes 196612
  9.2 11.8 %copy-start.4 = (bf16[2,128,512]{2,1,0:T(8,128)(2,1)S(1)}, bf16[2,128,512]{2,1,0:T(8,128)(2,1)}, u32[]{:S(2)}) copy-start(bf16[2,128,512]{2,1,0:T(8,128)(2,1)} %param.45) | copy-start | bytes 786436
  9.2 31.0 %all-to-all-start = ((bf16[4,16,128,128]{3,1,2,0:T(8,128)(2,1)}), bf16[4,16,128,128]{3,1,2,0:T(8,128)(2,1)}, u32[]{:S(2)}, u32[]{:S(2)}) async-start(bf16[4,16,128,128]{3,1,2,0:T(8,128)(2,1)} %copy_dynamic-update-slice_fusion.6), calls=%async_computation | async-start | bytes 4194304 | tf_op jit(solution)/shard_map/all_to_all | solution.py:205
  45.0 1.1 copy-start.15
  173.5 30.1 %all-to-all-start.1 = ((bf16[2,16,128,128]{3,1,0,2:T(8,128)(2,1)}), bf16[2,16,128,128]{3,1,0,2:T(8,128)(2,1)S(1)}, u32[]{:S(2)}, u32[]{:S(2)}) async-start(bf16[2,16,128,128]{3,1,0,2:T(8,128)(2,1)} %copy.338), calls=%async_computation.1 | async-start | bytes 2097152 | tf_op jit(solution)/shard_map/all_to_all | solution.py:149
  205.1 2.6 copy-start.10
  205.1 2.6 copy-start.11
  207.7 2.4 copy-start.16
  236.3 2.0 copy-start
  240.1 3.5 copy-start.6
  252.0 2.0 copy-start
  255.7 3.5 copy-start.6
  267.7 2.0 copy-start
  271.4 3.5 copy-start.6
  283.3 2.0 copy-start
  287.1 3.5 copy-start.6
  303.4 1.9 copy-start.1
  307.1 3.9 copy-start.7
  319.7 1.9 copy-start.1
  323.4 3.9 copy-start.7
  336.0 1.9 copy-start.1
  339.7 3.9 copy-start.7
  352.3 1.9 copy-start.1
  356.0 3.9 copy-start.7
  363.8 1.0 copy-start.3
  364.8 3.6 copy-start.2
  364.8 3.7 copy-start.8
  364.8 3.7 copy-start.9
  371.4 3.0 copy-start.17
where the time goes:
time: 536 us; the launch traced here: 531 us
  local copies, waits for them, and re-layouts  129 us (24%)
  loops' own time  109 us (20%)
  other arithmetic  88.3 us (16%)
  blocking collectives  85.6 us (16%)
  matrix products  60.5 us (11%)
  waiting for transfers between devices  44.9 us (8%)
  starting transfers between devices  9.02 us (2%)
    another operation x24, loops' own time, one_block(): return lax.cond(first_row + start < length, work, skipped, start)  76.6 us
    another operation x6, loops' own time, masked_blocks(): return lax.map(one_block, starts).reshape(rows_dev, width_all, chans)  31.1 us
    dynamic_slice x24, local copies, waits for them, and re-layouts, masked_blocks(): return lax.map(one_block, starts).reshape(rows_dev, width_all, chans)  30.2 us
    all_to_all x1, blocking collectives, transpose_pair(): lax.all_to_all(state, 'dap', split_axis=2, concat_axis=1, tiled=True)  29 us
    all_gather x2, blocking collectives, attend(): bias_all = lax.all_gather(bias_local, 'dap', axis=2, tiled=True)  28.9 us
    all_to_all x1, blocking collectives, on_device(): lax.all_to_all(homeward, 'grp', split_axis=0, concat_axis=0, tiled=True)  27.8 us
    all_to_all x1, waiting for transfers between devices, transpose_pair(): lax.all_to_all(state, 'dap', split_axis=2, concat_axis=1, tiled=True)  26.3 us
    dynamic_update_slice x24, local copies, waits for them, and re-layouts, masked_blocks(): return lax.map(one_block, starts).reshape(rows_dev, width_all, chans)  21.4 us
  transfers between devices with their start and end apart: 2, of which 2 were waited for; matrix products, arithmetic and copies ran while one was open for 1% of the time, Pallas kernels for 0%

commit v1 on v0

v1 whole, which is shorter than its diff:
```python
from functools import partial

import jax
import jax.numpy as jnp
from jax import lax
from jax.experimental import pallas as pl
from jax.experimental.pallas import tpu as pltpu
from jax.sharding import PartitionSpec as P

HEADS = 4
HEAD_DIM = 32
EPSILON = 1e-05
MASKED = -1e30
JBLOCK = 128

NT = (((1,), (1,)), ((), ()))


def layer_norm(values, gain_row, shift_row):
    values = values.astype(jnp.float32)
    center = values - jnp.mean(values, -1, keepdims=True)
    spread = jnp.mean(center * center, -1, keepdims=True)
    return (center * lax.rsqrt(spread + EPSILON) * gain_row + shift_row).astype(jnp.bfloat16)


def dot32(left, right):
    return jnp.dot(left, right, preferred_element_type=jnp.float32)


def kernel(
    dims,
    lens_ref,
    x_ref,
    gain_ref,
    shift_ref,
    proj_ref,
    wb_ref,
    wo_ref,
    up_ref,
    down_ref,
    out_ref,
    x1,
    y_s,
    q_s,
    k_s,
    v_s,
    g_s,
    tsc,
    bsc,
    bias_s,
    send_s,
    bias_send,
    bias_recv,
    flip_send,
    flip_recv,
):
    count, G, R, W, C, RB = dims
    me = lax.axis_index("dap")
    grp = lax.axis_index("grp")
    first_row = me * R
    my_cols = pl.ds(pl.multiple_of(first_row, R), R)

    barrier = pltpu.get_barrier_semaphore()

    def greet(d, carry):
        pl.semaphore_signal(
            barrier,
            inc=1,
            device_id=(grp, lax.rem(me + d, count)),
            device_id_type=pl.DeviceIdType.MESH,
        )
        return carry

    lax.fori_loop(1, count, greet, 0)

    lens = [lens_ref[grp * G + g] for g in range(G)]

    def bias_copy(m, g, d):
        return pltpu.make_async_remote_copy(
            src_ref=bias_s.at[m, me, g],
            dst_ref=bias_s.at[m, me, g],
            send_sem=bias_send.at[m, g, d],
            recv_sem=bias_recv.at[m, g, d],
            device_id=(grp, lax.rem(me + d, count)),
            device_id_type=pl.DeviceIdType.MESH,
        )

    def flip_copy(m, g, d):
        peer = lax.rem(me + d, count)
        land = x1 if m == 0 else out_ref
        return pltpu.make_async_remote_copy(
            src_ref=send_s.at[g, peer],
            dst_ref=land.at[g, :, my_cols, :],
            send_sem=flip_send.at[m, g, d],
            recv_sem=flip_recv.at[m, g, d],
            device_id=(grp, peer),
            device_id_type=pl.DeviceIdType.MESH,
        )

    def each_peer(act):
        def one(d, carry):
            act(d)
            return carry

        lax.fori_loop(1, count, one, 0)

    def norm_bias(m, g, src):
        gain = gain_ref[m : m + 1, :]
        shift = shift_ref[m : m + 1, :]

        def chunk(b, carry):
            rows = pl.ds(b * RB, RB)
            y = layer_norm(src[g, rows].reshape(RB * W, C), gain, shift)
            y_s[g, rows] = y.reshape(RB, W, C)
            bias = lax.dot_general(wb_ref[m], y, NT, preferred_element_type=jnp.float32)
            for rr in range(RB):
                bsc[b * RB + rr] = bias[:, rr * W : (rr + 1) * W]
            return carry

        lax.fori_loop(0, R // RB, chunk, 0)
        live = lax.broadcasted_iota(jnp.int32, (R, W), 1) < lens[g]
        for h in range(HEADS):
            bias_s[m, me, g, h] = jnp.where(live, bsc[:, h, :], MASKED).astype(jnp.bfloat16)

    def project(m, g):
        def chunk(b, carry):
            rows = pl.ds(b * RB, RB)
            y = y_s[g, rows].reshape(RB * W, C)
            p = dot32(y, proj_ref[m])
            q_s[rows] = (p[:, :C] * HEAD_DIM ** (-0.5)).astype(jnp.bfloat16).reshape(RB, W, C)
            k_s[rows] = p[:, C : 2 * C].astype(jnp.bfloat16).reshape(RB, W, C)
            v_s[rows] = p[:, 2 * C : 3 * C].astype(jnp.bfloat16).reshape(RB, W, C)
            g_s[rows] = jax.nn.sigmoid(p[:, 3 * C :]).reshape(RB, W, C)
            return carry

        lax.fori_loop(0, R // RB, chunk, 0)

    def row_mixed(m, g, r):
        head = lax.broadcasted_iota(jnp.int32, (JBLOCK, C), 1) // HEAD_DIM
        k = k_s[r]
        vext = jnp.concatenate([v_s[r], jnp.ones((W, C), jnp.bfloat16)], axis=1)
        per = JBLOCK // R
        parts = []
        for jb in range(W // JBLOCK):
            q = q_s[r, jb * JBLOCK : (jb + 1) * JBLOCK, :]
            stacked = jnp.concatenate(
                [jnp.where(head == h, q, jnp.zeros_like(q)) for h in range(HEADS)], axis=0
            )
            scores = lax.dot_general(stacked, k, NT, preferred_element_type=jnp.float32)
            weights = []
            for h in range(HEADS):
                bias = bias_s[m, jb * per : (jb + 1) * per, g, h].reshape(JBLOCK, W)
                s = scores[h * JBLOCK : (h + 1) * JBLOCK] + bias.astype(jnp.float32)
                top = jnp.max(s, -1, keepdims=True)
                weights.append(jnp.exp(s - top).astype(jnp.bfloat16))
            summed = dot32(jnp.concatenate(weights, axis=0), vext)
            num = summed[:JBLOCK, :C]
            den = summed[:JBLOCK, C:]
            for h in range(1, HEADS):
                at = slice(h * JBLOCK, (h + 1) * JBLOCK)
                num = jnp.where(head == h, summed[at, :C], num)
                den = jnp.where(head == h, summed[at, C:], den)
            parts.append(num / den)
        mixed = parts[0] if len(parts) == 1 else jnp.concatenate(parts, axis=0)
        return (mixed * g_s[r]).astype(jnp.bfloat16)

    def attend(m, g, src):
        col = lax.broadcasted_iota(jnp.int32, (W, C), 0)

        def live_of(r):
            return col < jnp.where(first_row + r < lens[g], lens[g], 0)

        def chunk(b, carry):
            gated = [row_mixed(m, g, b * RB + rr) for rr in range(RB)]
            joined = gated[0] if RB == 1 else jnp.concatenate(gated, axis=0)
            update = dot32(joined, wo_ref[m])
            done = []
            for rr in range(RB):
                r = b * RB + rr
                u = jnp.where(live_of(r), update[rr * W : (rr + 1) * W], 0.0)
                done.append((src[g, r].astype(jnp.float32) + u).astype(jnp.bfloat16))
            if m == 1:
                second = done[0] if RB == 1 else jnp.concatenate(done, axis=0)
                y = layer_norm(second, gain_ref[2:3, :], shift_ref[2:3, :])
                hidden = jnp.maximum(dot32(y, up_ref[...]), 0.0).astype(jnp.bfloat16)
                update = dot32(hidden, down_ref[...])
                for rr in range(RB):
                    r = b * RB + rr
                    u = jnp.where(live_of(r), update[rr * W : (rr + 1) * W], 0.0)
                    done[rr] = (done[rr].astype(jnp.float32) + u).astype(jnp.bfloat16)
            for rr in range(RB):
                tsc[:, b * RB + rr] = done[rr].astype(jnp.float32).reshape(W // R, R, C)
            return carry

        lax.fori_loop(0, R // RB, chunk, 0)

    def flip(m, g):
        if m == 1:
            each_peer(lambda d: flip_copy(0, g, d).wait_send())
        land = x1 if m == 0 else out_ref

        def one(d):
            peer = lax.rem(me + d, count)
            for c in range(R):
                send_s[g, peer, c] = tsc[peer, :, c, :].astype(jnp.bfloat16)
            flip_copy(m, g, d).start()

        each_peer(one)
        for c in range(R):
            land[g, c, my_cols, :] = tsc[me, :, c, :].astype(jnp.bfloat16)

    for g in range(G):
        norm_bias(0, g, x_ref)
        if g == 0:
            pl.semaphore_wait(barrier, count - 1)
        each_peer(lambda d: bias_copy(0, g, d).start())
    for g in range(G):
        project(0, g)
        each_peer(lambda d: bias_copy(0, g, d).wait_recv())
        attend(0, g, x_ref)
        flip(0, g)
    for g in range(G):
        each_peer(lambda d: flip_copy(0, g, d).wait_recv())
        norm_bias(1, g, x1)
        each_peer(lambda d: bias_copy(1, g, d).start())
    for g in range(G):
        project(1, g)
        each_peer(lambda d: bias_copy(1, g, d).wait_recv())
        attend(1, g, x1)
        flip(1, g)
    for g in range(G):
        each_peer(lambda d: flip_copy(1, g, d).wait())
        for m in range(2):
            each_peer(lambda d: bias_copy(m, g, d).wait_send())


def on_device(
    pair_state, lengths, norm_gain, norm_shift, attn_proj, bias_proj, attn_out, trans_up, trans_down
):
    G, R, W, C = pair_state.shape
    count = lax.axis_size("dap")
    RB = 4 if W <= 128 else 1
    wb = jnp.pad(jnp.swapaxes(bias_proj, 1, 2), ((0, 0), (0, 8 - HEADS), (0, 0)))
    bf = jnp.bfloat16
    f32 = jnp.float32
    vm = pl.BlockSpec(memory_space=pltpu.VMEM)
    return pl.pallas_call(
        partial(kernel, (count, G, R, W, C, RB)),
        out_shape=jax.ShapeDtypeStruct((G, R, W, C), bf),
        in_specs=[pl.BlockSpec(memory_space=pltpu.SMEM)] + [vm] * 8,
        out_specs=vm,
        scratch_shapes=[
            pltpu.VMEM((G, R, W, C), bf),
            pltpu.VMEM((G, R, W, C), bf),
            pltpu.VMEM((R, W, C), bf),
            pltpu.VMEM((R, W, C), bf),
            pltpu.VMEM((R, W, C), bf),
            pltpu.VMEM((R, W, C), f32),
            pltpu.VMEM((count, R, R, C), f32),
            pltpu.VMEM((R, 8, W), f32),
            pltpu.VMEM((2, count, G, HEADS, R, W), bf),
            pltpu.VMEM((G, count, R, R, C), bf),
            pltpu.SemaphoreType.DMA((2, G, count)),
            pltpu.SemaphoreType.DMA((2, G, count)),
            pltpu.SemaphoreType.DMA((2, G, count)),
            pltpu.SemaphoreType.DMA((2, G, count)),
        ],
        compiler_params=pltpu.CompilerParams(
            collective_id=0, has_side_effects=True, vmem_limit_bytes=60 * 1024 * 1024
        ),
        name="evoformer_pair",
    )(lengths, pair_state, norm_gain, norm_shift, attn_proj, wb, attn_out, trans_up, trans_down)


def solution(mesh):
    in_specs = (P("grp", "dap", None, None), P(), P(), P(), P(), P(), P(), P(), P())
    out_specs = P("grp", "dap", None, None)
    return jax.shard_map(
        on_device, mesh=mesh, in_specs=in_specs, out_specs=out_specs, check_vma=False
    )
```

time: 536 us -> 81.1 us (0.15)
  local copies, waits for them, and re-layouts: 129 us -> 3.59 us
  loops' own time: 109 us -> 0 us
  other arithmetic: 88.3 us -> 0 us
  blocking collectives: 85.6 us -> 0 us
  Pallas kernels: 0 us -> 76.3 us
  matrix products: 60.5 us -> 0 us
  waiting for transfers between devices: 44.9 us -> 0 us
  starting transfers between devices: 9.02 us -> 0 us
    another operation x46 -> x0, loops' own time: 109 us -> none  [the longest x24 76.6 us: one_block(): return lax.cond(first_row + start < length, work, skipped, start)]
    pallas_call x0 -> x1, Pallas kernels: none -> 76.3 us  [on_device(): pl.pallas_call(partial(kernel, (count, G, R, W, C, RB)), out_shape=jax.Sh...]
    dot_general x74 -> x0, matrix products: 60.5 us -> none  [the longest x16 16.7 us: row_update(): jnp.dot(gated.reshape(-1, chans), proj_out, preferred_element_type=jnp.fl...]
    all_to_all x2 -> x0, blocking collectives: 56.8 us -> none  [the longest x1 29 us: transpose_pair(): lax.all_to_all(state, 'dap', split_axis=2, concat_axis=1, tiled=True)]
    all_to_all x2 -> x0, waiting for transfers between devices: 44.9 us -> none  [the longest x1 26.3 us: transpose_pair(): lax.all_to_all(state, 'dap', split_axis=2, concat_axis=1, tiled=True)]
    lt x64 -> x0, other arithmetic: 44.6 us -> none  [the longest x24 19.8 us: masked_blocks(): col_live = jnp.arange(width_all, dtype=jnp.int32) < length]
    dynamic_slice x35 -> x0, local copies, waits for them, and re-layouts: 39.1 us -> none  [the longest x24 30.2 us: masked_blocks(): return lax.map(one_block, starts).reshape(rows_dev, width_all, chans)]
    all_gather x2 -> x0, blocking collectives: 28.9 us -> none  [attend(): bias_all = lax.all_gather(bias_local, 'dap', axis=2, tiled=True)]
  transfers between devices with their start and end apart: 2 -> 0, of which waited for: 2 -> 0; matrix products, arithmetic and copies ran while one was open for 1% -> 0% of each run, Pallas kernels for 0% -> 0%
where the time goes in v1:
time: 81.1 us; the launch traced here: 79.9 us
  Pallas kernels  76.3 us (94%)
  local copies, waits for them, and re-layouts  3.59 us (4%)
    pallas_call x1, Pallas kernels, on_device(): pl.pallas_call(partial(kernel, (count, G, R, W, C, RB)), out_shape=jax.Sh...  76.3 us
    unnamed x1, local copies, waits for them, and re-layouts  2.31 us

profile of v1, /device:TPU:0, one launch (start us, length us, event | category | flops | bytes accessed | tf_op | source)
XLA Modules:
  0.0 79.9 jit_solution(17590492672633098917)
XLA Ops:
  0.0 1.3 %pad.4.wb_ref = bf16[2,8,128]{2,1,0:T(8,128)(2,1)} pad(bf16[2,4,128]{2,1,0:T(4,128)(2,1)} %bitcast.1, bf16[]{:T(256)} %constant.2.clone.1), padding=0_0x0_4x0_0 | pad | bytes 6146 | tf_op jit(solution)/shard_map/jit(_pad)/pad | solution.py:243
  1.3 76.3 %evoformer_pair.1 = bf16[2,16,128,128]{3,2,1,0:T(8,128)(2,1)} custom-call(s32[8]{0:T(128)} %lens_ref.1, bf16[2,16,128,128]{3,2,1,0:T(8,128)(2,1)} %x_ref.1, f32[3,128]{1,0:T(4,128)} %gain_ref.1, f32[3,128]{1,0:T(4,128)} %shift_ref.1, bf16[2,128,512]{2,1,0:T(8,128)(2,1)} %proj_ref.1, bf16[2,8,128]{2,1,0:T(8,128)(2,1)} %pad.4.wb_ref, ...), custom_call_target="tpu_custom_call" | custom-call | tf_op jit(solution)/shard_map/evoformer_pair/pallas_call | solution.py:247
  77.5 2.3 %copy.11 = bf16[2,16,128,128]{3,2,1,0:T(8,128)(2,1)} copy(bf16[2,16,128,128]{3,2,1,0:T(8,128)(2,1)} %evoformer_pair.1) | data formatting | bytes 2097152

commit v2 on v1

--- a/solution.py
+++ b/solution.py
@@ -40,6 +40,7 @@
     down_ref,
     out_ref,
     x1,
+    landed,
     y_s,
     q_s,
     k_s,
@@ -58,7 +59,6 @@
     me = lax.axis_index("dap")
     grp = lax.axis_index("grp")
     first_row = me * R
-    my_cols = pl.ds(pl.multiple_of(first_row, R), R)
 
     barrier = pltpu.get_barrier_semaphore()
 
@@ -85,12 +85,11 @@
             device_id_type=pl.DeviceIdType.MESH,
         )
 
-    def flip_copy(m, g, d):
+    def flip_copy(m, g, d, start, size):
         peer = lax.rem(me + d, count)
-        land = x1 if m == 0 else out_ref
         return pltpu.make_async_remote_copy(
-            src_ref=send_s.at[g, peer],
-            dst_ref=land.at[g, :, my_cols, :],
+            src_ref=send_s.at[g, pl.ds(start, size), peer],
+            dst_ref=landed.at[m, g, pl.ds(first_row + start, size)],
             send_sem=flip_send.at[m, g, d],
             recv_sem=flip_recv.at[m, g, d],
             device_id=(grp, peer),
@@ -102,17 +101,26 @@
             act(d)
             return carry
 
-        lax.fori_loop(1, count, one, 0)
+        lax.fori_loop(1, count, one, 0, unroll=count <= 8)
 
     def norm_bias(m, g, src):
         gain = gain_ref[m : m + 1, :]
         shift = shift_ref[m : m + 1, :]
+        pick = lax.broadcasted_iota(jnp.int32, (8, HEADS), 0) == lax.broadcasted_iota(
+            jnp.int32, (8, HEADS), 1
+        )
+        wb = lax.dot_general(
+            jnp.where(pick, 1.0, 0.0).astype(jnp.bfloat16),
+            wb_ref[m],
+            NT,
+            preferred_element_type=jnp.float32,
+        ).astype(jnp.bfloat16)
 
         def chunk(b, carry):
             rows = pl.ds(b * RB, RB)
             y = layer_norm(src[g, rows].reshape(RB * W, C), gain, shift)
             y_s[g, rows] = y.reshape(RB, W, C)
-            bias = lax.dot_general(wb_ref[m], y, NT, preferred_element_type=jnp.float32)
+            bias = lax.dot_general(wb, y, NT, preferred_element_type=jnp.float32)
             for rr in range(RB):
                 bsc[b * RB + rr] = bias[:, rr * W : (rr + 1) * W]
             return carry
@@ -189,25 +197,25 @@
                     u = jnp.where(live_of(r), update[rr * W : (rr + 1) * W], 0.0)
                     done[rr] = (done[rr].astype(jnp.float32) + u).astype(jnp.bfloat16)
             for rr in range(RB):
-                tsc[:, b * RB + rr] = done[rr].astype(jnp.float32).reshape(W // R, R, C)
+                r = b * RB + rr
+                send_s[g, r] = done[rr].reshape(count, R, C)
+                landed[m, g, first_row + r] = send_s[g, r, me]
+            each_peer(lambda d: flip_copy(m, g, d, b * RB, RB).start())
             return carry
 
         lax.fori_loop(0, R // RB, chunk, 0)
 
-    def flip(m, g):
-        if m == 1:
-            each_peer(lambda d: flip_copy(0, g, d).wait_send())
-        land = x1 if m == 0 else out_ref
-
-        def one(d):
-            peer = lax.rem(me + d, count)
+    def gather_flip(m, g, target):
+        each_peer(lambda d: flip_copy(m, g, d, 0, R).wait_recv())
+
+        def one(p, carry):
+            rows = pl.ds(pl.multiple_of(p * R, R), R)
+            tsc[p] = landed[m, g, rows].astype(jnp.float32)
             for c in range(R):
-                send_s[g, peer, c] = tsc[peer, :, c, :].astype(jnp.bfloat16)
-            flip_copy(m, g, d).start()
-
-        each_peer(one)
-        for c in range(R):
-            land[g, c, my_cols, :] = tsc[me, :, c, :].astype(jnp.bfloat16)
+                target[g, c, rows, :] = tsc[p, :, c, :].astype(jnp.bfloat16)
+            return carry
+
+        lax.fori_loop(0, count, one, 0, unroll=count <= 8)
 
     for g in range(G):
         norm_bias(0, g, x_ref)
@@ -218,18 +226,23 @@
         project(0, g)
         each_peer(lambda d: bias_copy(0, g, d).wait_recv())
         attend(0, g, x_ref)
-        flip(0, g)
-    for g in range(G):
-        each_peer(lambda d: flip_copy(0, g, d).wait_recv())
+    gather_flip(0, 0, x1)
+    norm_bias(1, 0, x1)
+    each_peer(lambda d: bias_copy(1, 0, d).start())
+    project(1, 0)
+    for g in range(1, G):
+        gather_flip(0, g, x1)
         norm_bias(1, g, x1)
         each_peer(lambda d: bias_copy(1, g, d).start())
     for g in range(G):
-        project(1, g)
+        if g > 0:
+            project(1, g)
         each_peer(lambda d: bias_copy(1, g, d).wait_recv())
+        each_peer(lambda d: flip_copy(0, g, d, 0, R).wait_send())
         attend(1, g, x1)
-        flip(1, g)
-    for g in range(G):
-        each_peer(lambda d: flip_copy(1, g, d).wait())
+    for g in range(G):
+        gather_flip(1, g, out_ref)
+        each_peer(lambda d: flip_copy(1, g, d, 0, R).wait_send())
         for m in range(2):
             each_peer(lambda d: bias_copy(m, g, d).wait_send())
 
@@ -240,7 +253,6 @@
     G, R, W, C = pair_state.shape
     count = lax.axis_size("dap")
     RB = 4 if W <= 128 else 1
-    wb = jnp.pad(jnp.swapaxes(bias_proj, 1, 2), ((0, 0), (0, 8 - HEADS), (0, 0)))
     bf = jnp.bfloat16
     f32 = jnp.float32
     vm = pl.BlockSpec(memory_space=pltpu.VMEM)
@@ -251,6 +263,7 @@
         out_specs=vm,
         scratch_shapes=[
             pltpu.VMEM((G, R, W, C), bf),
+            pltpu.VMEM((2, G, W, R, C), bf),
             pltpu.VMEM((G, R, W, C), bf),
             pltpu.VMEM((R, W, C), bf),
             pltpu.VMEM((R, W, C), bf),
@@ -259,7 +272,7 @@
             pltpu.VMEM((count, R, R, C), f32),
             pltpu.VMEM((R, 8, W), f32),
             pltpu.VMEM((2, count, G, HEADS, R, W), bf),
-            pltpu.VMEM((G, count, R, R, C), bf),
+            pltpu.VMEM((G, R, count, R, C), bf),
             pltpu.SemaphoreType.DMA((2, G, count)),
             pltpu.SemaphoreType.DMA((2, G, count)),
             pltpu.SemaphoreType.DMA((2, G, count)),
@@ -269,7 +282,7 @@
             collective_id=0, has_side_effects=True, vmem_limit_bytes=60 * 1024 * 1024
         ),
         name="evoformer_pair",
-    )(lengths, pair_state, norm_gain, norm_shift, attn_proj, wb, attn_out, trans_up, trans_down)
+    )(lengths, pair_state, norm_gain, norm_shift, attn_proj, bias_proj, attn_out, trans_up, trans_down)
 
 
 def solution(mesh):

time: 81.1 us -> 74.6 us (0.920); the launches traced: 79.9 us -> 74.4 us
  Pallas kernels: 76.3 us -> 70.7 us
    pallas_call x1, Pallas kernels: 76.3 us -> 70.7 us  [on_device(): pl.pallas_call(partial(kernel, (count, G, R, W, C, RB)), out_shape=jax.Sh...]
    unnamed x1 -> x2, local copies, waits for them, and re-layouts: 2.31 us -> 3.74 us
    pad x1 -> x0, local copies, waits for them, and re-layouts: 1.28 us -> none  [on_device(): jnp.pad(jnp.swapaxes(bias_proj, 1, 2), ((0, 0), (0, 8 - HEADS), (0, 0)))]
where the time goes in v2:
time: 74.6 us; the launch traced here: 74.4 us
  Pallas kernels  70.7 us (95%)
  local copies, waits for them, and re-layouts  3.74 us (5%)
    pallas_call x1, Pallas kernels, on_device(): pl.pallas_call(partial(kernel, (count, G, R, W, C, RB)), out_shape=jax.Sh...  70.7 us
    unnamed x2, local copies, waits for them, and re-layouts  3.74 us

profile of v2, /device:TPU:0, one launch (start us, length us, event | category | flops | bytes accessed | tf_op | source)
XLA Modules:
  0.0 74.4 jit_solution(5262932742987704728)
XLA Ops:
  0.0 1.4 %copy.10.wb_ref = bf16[2,128,4]{2,1,0:T(8,128)(2,1)} copy(bf16[2,128,4]{1,2,0:T(4,128)(2,1)} %param.14) | data formatting | bytes 4096 | tf_op args[5]
  1.4 70.7 %evoformer_pair.1 = bf16[2,16,128,128]{3,2,1,0:T(8,128)(2,1)} custom-call(s32[8]{0:T(128)} %lens_ref.1, bf16[2,16,128,128]{3,2,1,0:T(8,128)(2,1)} %x_ref.1, f32[3,128]{1,0:T(4,128)} %gain_ref.1, f32[3,128]{1,0:T(4,128)} %shift_ref.1, bf16[2,128,512]{2,1,0:T(8,128)(2,1)} %proj_ref.1, bf16[2,128,4]{2,1,0:T(8,128)(2,1)} %copy.10.wb_ref, ...), custom_call_target="tpu_custom_call" | custom-call | tf_op jit(solution)/shard_map/evoformer_pair/pallas_call | solution.py:259
  72.1 2.3 %copy.12 = bf16[2,16,128,128]{3,2,1,0:T(8,128)(2,1)} copy(bf16[2,16,128,128]{3,2,1,0:T(8,128)(2,1)} %evoformer_pair.1) | data formatting | bytes 2097152

commit v3 on v2

--- a/solution.py
+++ b/solution.py
@@ -48,6 +48,7 @@
     g_s,
     tsc,
     bsc,
+    bias_t,
     bias_s,
     send_s,
     bias_send,
@@ -73,7 +74,26 @@
 
     lax.fori_loop(1, count, greet, 0)
 
-    lens = [lens_ref[grp * G + g] for g in range(G)]
+    pick = lax.broadcasted_iota(jnp.int32, (8, HEADS), 0) == lax.broadcasted_iota(
+        jnp.int32, (8, HEADS), 1
+    )
+    pick = jnp.where(pick, 1.0, 0.0).astype(jnp.bfloat16)
+
+    def length_of(g):
+        return lens_ref[grp * G + g]
+
+    def head_weights(m):
+        return dot32(pick, wb_ref[m]).astype(jnp.bfloat16)
+
+    def put_bias(weights, y, b):
+        bias = lax.dot_general(weights, y, NT, preferred_element_type=jnp.float32)
+        for rr in range(RB):
+            bsc[b * RB + rr] = bias[:, rr * W : (rr + 1) * W]
+
+    def send_bias(m, g, live):
+        for h in range(HEADS):
+            bias_s[m, me, g, h] = jnp.where(live, bsc[:, h, :], MASKED).astype(jnp.bfloat16)
+        each_peer(lambda d: bias_copy(m, g, d).start())
 
     def bias_copy(m, g, d):
         return pltpu.make_async_remote_copy(
@@ -103,37 +123,27 @@
 
         lax.fori_loop(1, count, one, 0, unroll=count <= 8)
 
-    def norm_bias(m, g, src):
-        gain = gain_ref[m : m + 1, :]
-        shift = shift_ref[m : m + 1, :]
-        pick = lax.broadcasted_iota(jnp.int32, (8, HEADS), 0) == lax.broadcasted_iota(
-            jnp.int32, (8, HEADS), 1
-        )
-        wb = lax.dot_general(
-            jnp.where(pick, 1.0, 0.0).astype(jnp.bfloat16),
-            wb_ref[m],
-            NT,
-            preferred_element_type=jnp.float32,
-        ).astype(jnp.bfloat16)
+    def norm_bias(g):
+        weights = head_weights(0)
 
         def chunk(b, carry):
             rows = pl.ds(b * RB, RB)
-            y = layer_norm(src[g, rows].reshape(RB * W, C), gain, shift)
+            y = layer_norm(x_ref[g, rows].reshape(RB * W, C), gain_ref[0:1, :], shift_ref[0:1, :])
             y_s[g, rows] = y.reshape(RB, W, C)
-            bias = lax.dot_general(wb, y, NT, preferred_element_type=jnp.float32)
-            for rr in range(RB):
-                bsc[b * RB + rr] = bias[:, rr * W : (rr + 1) * W]
+            put_bias(weights, y, b)
             return carry
 
         lax.fori_loop(0, R // RB, chunk, 0)
-        live = lax.broadcasted_iota(jnp.int32, (R, W), 1) < lens[g]
-        for h in range(HEADS):
-            bias_s[m, me, g, h] = jnp.where(live, bsc[:, h, :], MASKED).astype(jnp.bfloat16)
 
     def project(m, g):
         def chunk(b, carry):
             rows = pl.ds(b * RB, RB)
-            y = y_s[g, rows].reshape(RB * W, C)
+            if m == 0:
+                y = y_s[g, rows].reshape(RB * W, C)
+            else:
+                y = layer_norm(
+                    x1[g, rows].reshape(RB * W, C), gain_ref[1:2, :], shift_ref[1:2, :]
+                )
             p = dot32(y, proj_ref[m])
             q_s[rows] = (p[:, :C] * HEAD_DIM ** (-0.5)).astype(jnp.bfloat16).reshape(RB, W, C)
             k_s[rows] = p[:, C : 2 * C].astype(jnp.bfloat16).reshape(RB, W, C)
@@ -142,6 +152,15 @@
             return carry
 
         lax.fori_loop(0, R // RB, chunk, 0)
+
+    def turn_bias(g):
+        per = JBLOCK // R
+        for h in range(HEADS):
+            for kb in range(W // JBLOCK):
+                part = bias_s[1, kb * per : (kb + 1) * per, g, h].reshape(JBLOCK, W)
+                bias_t[h, :, kb * JBLOCK : (kb + 1) * JBLOCK] = part.astype(jnp.float32).T.astype(
+                    jnp.bfloat16
+                )
 
     def row_mixed(m, g, r):
         head = lax.broadcasted_iota(jnp.int32, (JBLOCK, C), 1) // HEAD_DIM
@@ -157,7 +176,10 @@
             scores = lax.dot_general(stacked, k, NT, preferred_element_type=jnp.float32)
             weights = []
             for h in range(HEADS):
-                bias = bias_s[m, jb * per : (jb + 1) * per, g, h].reshape(JBLOCK, W)
+                if m == 0:
+                    bias = bias_s[0, jb * per : (jb + 1) * per, g, h].reshape(JBLOCK, W)
+                else:
+                    bias = bias_t[h, jb * JBLOCK : (jb + 1) * JBLOCK, :]
                 s = scores[h * JBLOCK : (h + 1) * JBLOCK] + bias.astype(jnp.float32)
                 top = jnp.max(s, -1, keepdims=True)
                 weights.append(jnp.exp(s - top).astype(jnp.bfloat16))
@@ -174,9 +196,11 @@
 
     def attend(m, g, src):
         col = lax.broadcasted_iota(jnp.int32, (W, C), 0)
+        length = length_of(g)
+        weights = head_weights(1)
 
         def live_of(r):
-            return col < jnp.where(first_row + r < lens[g], lens[g], 0)
+            return col < jnp.where(first_row + r < length, length, 0)
 
         def chunk(b, carry):
             gated = [row_mixed(m, g, b * RB + rr) for rr in range(RB)]
@@ -201,6 +225,9 @@
                 send_s[g, r] = done[rr].reshape(count, R, C)
                 landed[m, g, first_row + r] = send_s[g, r, me]
             each_peer(lambda d: flip_copy(m, g, d, b * RB, RB).start())
+            if m == 0:
+                first = done[0] if RB == 1 else jnp.concatenate(done, axis=0)
+                put_bias(weights, layer_norm(first, gain_ref[1:2, :], shift_ref[1:2, :]), b)
             return carry
 
         lax.fori_loop(0, R // RB, chunk, 0)
@@ -217,34 +244,44 @@
 
         lax.fori_loop(0, count, one, 0, unroll=count <= 8)
 
-    for g in range(G):
-        norm_bias(0, g, x_ref)
-        if g == 0:
+    column = lax.broadcasted_iota(jnp.int32, (R, W), 1)
+    row = lax.broadcasted_iota(jnp.int32, (R, W), 0) + first_row
+
+    def begin(g, carry):
+        norm_bias(g)
+
+        @pl.when(g == 0)
+        def _():
             pl.semaphore_wait(barrier, count - 1)
-        each_peer(lambda d: bias_copy(0, g, d).start())
-    for g in range(G):
+
+        send_bias(0, g, column < length_of(g))
+        return carry
+
+    def start_node(g, carry):
         project(0, g)
         each_peer(lambda d: bias_copy(0, g, d).wait_recv())
         attend(0, g, x_ref)
-    gather_flip(0, 0, x1)
-    norm_bias(1, 0, x1)
-    each_peer(lambda d: bias_copy(1, 0, d).start())
-    project(1, 0)
-    for g in range(1, G):
+        send_bias(1, g, row < length_of(g))
+        return carry
+
+    def end_node(g, carry):
         gather_flip(0, g, x1)
-        norm_bias(1, g, x1)
-        each_peer(lambda d: bias_copy(1, g, d).start())
-    for g in range(G):
-        if g > 0:
-            project(1, g)
+        project(1, g)
         each_peer(lambda d: bias_copy(1, g, d).wait_recv())
+        turn_bias(g)
         each_peer(lambda d: flip_copy(0, g, d, 0, R).wait_send())
         attend(1, g, x1)
-    for g in range(G):
+        return carry
+
+    def finish(g, carry):
         gather_flip(1, g, out_ref)
         each_peer(lambda d: flip_copy(1, g, d, 0, R).wait_send())
         for m in range(2):
             each_peer(lambda d: bias_copy(m, g, d).wait_send())
+        return carry
+
+    for stage in (begin, start_node, end_node, finish):
+        lax.fori_loop(0, G, stage, 0)
 
 
 def on_device(
@@ -253,6 +290,7 @@
     G, R, W, C = pair_state.shape
     count = lax.axis_size("dap")
     RB = 4 if W <= 128 else 1
+    wb = jnp.swapaxes(bias_proj, 1, 2)
     bf = jnp.bfloat16
     f32 = jnp.float32
     vm = pl.BlockSpec(memory_space=pltpu.VMEM)
@@ -271,6 +309,7 @@
             pltpu.VMEM((R, W, C), f32),
             pltpu.VMEM((count, R, R, C), f32),
             pltpu.VMEM((R, 8, W), f32),
+            pltpu.VMEM((HEADS, W, W), bf),
             pltpu.VMEM((2, count, G, HEADS, R, W), bf),
             pltpu.VMEM((G, R, count, R, C), bf),
             pltpu.SemaphoreType.DMA((2, G, count)),
@@ -282,7 +321,7 @@
             collective_id=0, has_side_effects=True, vmem_limit_bytes=60 * 1024 * 1024
         ),
         name="evoformer_pair",
-    )(lengths, pair_state, norm_gain, norm_shift, attn_proj, bias_proj, attn_out, trans_up, trans_down)
+    )(lengths, pair_state, norm_gain, norm_shift, attn_proj, wb, attn_out, trans_up, trans_down)
 
 
 def solution(mesh):

time: 74.6 us -> 70.5 us (0.945)
  Pallas kernels: 70.7 us -> 68 us
  local copies, waits for them, and re-layouts: 3.74 us -> 2.31 us
    pallas_call x1, Pallas kernels: 70.7 us -> 68 us  [on_device(): pl.pallas_call(partial(kernel, (count, G, R, W, C, RB)), out_shape=jax.Sh...]
    unnamed x2 -> x1, local copies, waits for them, and re-layouts: 3.74 us -> 2.31 us
where the time goes in v3:
time: 70.5 us; the launch traced here: 70.4 us
  Pallas kernels  68 us (96%)
  local copies, waits for them, and re-layouts  2.31 us (3%)
    pallas_call x1, Pallas kernels, on_device(): pl.pallas_call(partial(kernel, (count, G, R, W, C, RB)), out_shape=jax.Sh...  68 us
    unnamed x1, local copies, waits for them, and re-layouts  2.31 us

profile of v3, /device:TPU:0, one launch (start us, length us, event | category | flops | bytes accessed | tf_op | source)
XLA Modules:
  0.0 70.4 jit_solution(8809729320940218)
XLA Ops:
  0.0 68.0 %evoformer_pair.1 = bf16[2,16,128,128]{3,2,1,0:T(8,128)(2,1)} custom-call(s32[8]{0:T(128)} %lens_ref.1, bf16[2,16,128,128]{3,2,1,0:T(8,128)(2,1)} %x_ref.1, f32[3,128]{1,0:T(4,128)} %gain_ref.1, f32[3,128]{1,0:T(4,128)} %shift_ref.1, bf16[2,128,512]{2,1,0:T(8,128)(2,1)} %proj_ref.1, bf16[2,4,128]{2,1,0:T(4,128)(2,1)} %bitcast.1, ...), custom_call_target="tpu_custom_call" | custom-call | tf_op jit(solution)/shard_map/evoformer_pair/pallas_call | solution.py:297
  68.0 2.3 %copy.11 = bf16[2,16,128,128]{3,2,1,0:T(8,128)(2,1)} copy(bf16[2,16,128,128]{3,2,1,0:T(8,128)(2,1)} %evoformer_pair.1) | data formatting | bytes 2097152

commit v4 on v3

--- a/solution.py
+++ b/solution.py
@@ -17,9 +17,17 @@
 
 
 def layer_norm(values, gain_row, shift_row):
-    values = values.astype(jnp.float32)
-    center = values - jnp.mean(values, -1, keepdims=True)
-    spread = jnp.mean(center * center, -1, keepdims=True)
+    chans = values.shape[-1]
+    center = values.astype(jnp.float32) - dot32(
+        values, jnp.full((chans, chans), 1.0 / chans, jnp.bfloat16)
+    )
+    square = center * center
+    high = square.astype(jnp.bfloat16)
+    low = (square - high.astype(jnp.float32)).astype(jnp.bfloat16)
+    spread = dot32(
+        jnp.concatenate([high, low], axis=-1),
+        jnp.full((2 * chans, chans), 1.0 / chans, jnp.bfloat16),
+    )
     return (center * lax.rsqrt(spread + EPSILON) * gain_row + shift_row).astype(jnp.bfloat16)
 
 
@@ -49,6 +57,7 @@
     tsc,
     bsc,
     bias_t,
+    turned_s,
     bias_s,
     send_s,
     bias_send,
@@ -144,11 +153,16 @@
                 y = layer_norm(
                     x1[g, rows].reshape(RB * W, C), gain_ref[1:2, :], shift_ref[1:2, :]
                 )
-            p = dot32(y, proj_ref[m])
-            q_s[rows] = (p[:, :C] * HEAD_DIM ** (-0.5)).astype(jnp.bfloat16).reshape(RB, W, C)
-            k_s[rows] = p[:, C : 2 * C].astype(jnp.bfloat16).reshape(RB, W, C)
-            v_s[rows] = p[:, 2 * C : 3 * C].astype(jnp.bfloat16).reshape(RB, W, C)
-            g_s[rows] = jax.nn.sigmoid(p[:, 3 * C :]).reshape(RB, W, C)
+            k_s[rows] = (
+                dot32(y, proj_ref[m, :, C : 2 * C]).astype(jnp.bfloat16).reshape(RB, W, C)
+            )
+            p = lax.dot_general(turned_s[m], y, NT, preferred_element_type=jnp.float32)
+            for rr in range(RB):
+                r = b * RB + rr
+                at = slice(rr * W, (rr + 1) * W)
+                q_s[r] = (p[:C, at] * HEAD_DIM ** (-0.5)).astype(jnp.bfloat16)
+                v_s[r] = p[C : 2 * C, at].astype(jnp.bfloat16)
+                g_s[r] = jax.nn.sigmoid(p[2 * C :, at])
             return carry
 
         lax.fori_loop(0, R // RB, chunk, 0)
@@ -157,42 +171,43 @@
         per = JBLOCK // R
         for h in range(HEADS):
             for kb in range(W // JBLOCK):
-                part = bias_s[1, kb * per : (kb + 1) * per, g, h].reshape(JBLOCK, W)
+                part = bias_s[0, kb * per : (kb + 1) * per, g, h].reshape(JBLOCK, W)
                 bias_t[h, :, kb * JBLOCK : (kb + 1) * JBLOCK] = part.astype(jnp.float32).T.astype(
                     jnp.bfloat16
                 )
 
-    def row_mixed(m, g, r):
-        head = lax.broadcasted_iota(jnp.int32, (JBLOCK, C), 1) // HEAD_DIM
+    def row_gated(m, g, r):
         k = k_s[r]
-        vext = jnp.concatenate([v_s[r], jnp.ones((W, C), jnp.bfloat16)], axis=1)
-        per = JBLOCK // R
-        parts = []
+        rows = []
         for jb in range(W // JBLOCK):
-            q = q_s[r, jb * JBLOCK : (jb + 1) * JBLOCK, :]
-            stacked = jnp.concatenate(
-                [jnp.where(head == h, q, jnp.zeros_like(q)) for h in range(HEADS)], axis=0
+            at = slice(jb * JBLOCK, (jb + 1) * JBLOCK)
+            q = q_s[r, :, at]
+            head = lax.broadcasted_iota(jnp.int32, (C, JBLOCK), 0) // HEAD_DIM
+            spread = jnp.concatenate(
+                [jnp.where(head == h, q, jnp.zeros_like(q)) for h in range(HEADS)], axis=1
             )
-            scores = lax.dot_general(stacked, k, NT, preferred_element_type=jnp.float32)
-            weights = []
+            scores = dot32(k, spread)
+            parts = []
             for h in range(HEADS):
                 if m == 0:
-                    bias = bias_s[0, jb * per : (jb + 1) * per, g, h].reshape(JBLOCK, W)
+                    bias = bias_t[h, :, at]
                 else:
-                    bias = bias_t[h, jb * JBLOCK : (jb + 1) * JBLOCK, :]
-                s = scores[h * JBLOCK : (h + 1) * JBLOCK] + bias.astype(jnp.float32)
-                top = jnp.max(s, -1, keepdims=True)
-                weights.append(jnp.exp(s - top).astype(jnp.bfloat16))
-            summed = dot32(jnp.concatenate(weights, axis=0), vext)
-            num = summed[:JBLOCK, :C]
-            den = summed[:JBLOCK, C:]
-            for h in range(1, HEADS):
-                at = slice(h * JBLOCK, (h + 1) * JBLOCK)
-                num = jnp.where(head == h, summed[at, :C], num)
-                den = jnp.where(head == h, summed[at, C:], den)
-            parts.append(num / den)
-        mixed = parts[0] if len(parts) == 1 else jnp.concatenate(parts, axis=0)
-        return (mixed * g_s[r]).astype(jnp.bfloat16)
+                    bias = bias_s[1, :, g, h, :, at].reshape(W, JBLOCK)
+                s = scores[:, h * JBLOCK : (h + 1) * JBLOCK] + bias.astype(jnp.float32)
+                top = jnp.max(s, 0, keepdims=True)
+                weights = jnp.exp(s - top).astype(jnp.bfloat16)
+                left = jnp.concatenate(
+                    [
+                        v_s[r, h * HEAD_DIM : (h + 1) * HEAD_DIM, :],
+                        jnp.ones((16, W), jnp.bfloat16),
+                    ],
+                    axis=0,
+                )
+                summed = dot32(left, weights)
+                parts.append(summed[:HEAD_DIM] / summed[HEAD_DIM : HEAD_DIM + 1])
+            gated = jnp.concatenate(parts, axis=0) * g_s[r, :, at]
+            rows.append(gated.T.astype(jnp.bfloat16))
+        return rows[0] if len(rows) == 1 else jnp.concatenate(rows, axis=0)
 
     def attend(m, g, src):
         col = lax.broadcasted_iota(jnp.int32, (W, C), 0)
@@ -203,7 +218,7 @@
             return col < jnp.where(first_row + r < length, length, 0)
 
         def chunk(b, carry):
-            gated = [row_mixed(m, g, b * RB + rr) for rr in range(RB)]
+            gated = [row_gated(m, g, b * RB + rr) for rr in range(RB)]
             joined = gated[0] if RB == 1 else jnp.concatenate(gated, axis=0)
             update = dot32(joined, wo_ref[m])
             done = []
@@ -260,6 +275,7 @@
     def start_node(g, carry):
         project(0, g)
         each_peer(lambda d: bias_copy(0, g, d).wait_recv())
+        turn_bias(g)
         attend(0, g, x_ref)
         send_bias(1, g, row < length_of(g))
         return carry
@@ -268,7 +284,6 @@
         gather_flip(0, g, x1)
         project(1, g)
         each_peer(lambda d: bias_copy(1, g, d).wait_recv())
-        turn_bias(g)
         each_peer(lambda d: flip_copy(0, g, d, 0, R).wait_send())
         attend(1, g, x1)
         return carry
@@ -280,6 +295,10 @@
             each_peer(lambda d: bias_copy(m, g, d).wait_send())
         return carry
 
+    for m in range(2):
+        for at, first in enumerate((0, 2 * C, 3 * C)):
+            part = proj_ref[m, :, first : first + C].astype(jnp.float32)
+            turned_s[m, at * C : (at + 1) * C, :] = part.T.astype(jnp.bfloat16)
     for stage in (begin, start_node, end_node, finish):
         lax.fori_loop(0, G, stage, 0)
 
@@ -303,13 +322,14 @@
             pltpu.VMEM((G, R, W, C), bf),
             pltpu.VMEM((2, G, W, R, C), bf),
             pltpu.VMEM((G, R, W, C), bf),
+            pltpu.VMEM((R, C, W), bf),
             pltpu.VMEM((R, W, C), bf),
-            pltpu.VMEM((R, W, C), bf),
-            pltpu.VMEM((R, W, C), bf),
-            pltpu.VMEM((R, W, C), f32),
+            pltpu.VMEM((R, C, W), bf),
+            pltpu.VMEM((R, C, W), f32),
             pltpu.VMEM((count, R, R, C), f32),
             pltpu.VMEM((R, 8, W), f32),
             pltpu.VMEM((HEADS, W, W), bf),
+            pltpu.VMEM((2, 3 * C, C), bf),
             pltpu.VMEM((2, count, G, HEADS, R, W), bf),
             pltpu.VMEM((G, R, count, R, C), bf),
             pltpu.SemaphoreType.DMA((2, G, count)),

time: 70.5 us -> 70.8 us (level)
  no operation moved by 1% of the time
where the time goes in v4:
time: 70.8 us; the launch traced here: 70.6 us
  Pallas kernels  68.3 us (96%)
  local copies, waits for them, and re-layouts  2.31 us (3%)
    pallas_call x1, Pallas kernels, on_device(): pl.pallas_call(partial(kernel, (count, G, R, W, C, RB)), out_shape=jax.Sh...  68.3 us
    unnamed x1, local copies, waits for them, and re-layouts  2.31 us

profile of v4, /device:TPU:0, one launch (start us, length us, event | category | flops | bytes accessed | tf_op | source)
XLA Modules:
  0.0 70.6 jit_solution(11601557326253668357)
XLA Ops:
  0.0 68.3 %evoformer_pair.1 = bf16[2,16,128,128]{3,2,1,0:T(8,128)(2,1)} custom-call(s32[8]{0:T(128)} %lens_ref.1, bf16[2,16,128,128]{3,2,1,0:T(8,128)(2,1)} %x_ref.1, f32[3,128]{1,0:T(4,128)} %gain_ref.1, f32[3,128]{1,0:T(4,128)} %shift_ref.1, bf16[2,128,512]{2,1,0:T(8,128)(2,1)} %proj_ref.1, bf16[2,4,128]{2,1,0:T(4,128)(2,1)} %bitcast.1, ...), custom_call_target="tpu_custom_call" | custom-call | tf_op jit(solution)/shard_map/evoformer_pair/pallas_call | solution.py:316
  68.3 2.3 %copy.11 = bf16[2,16,128,128]{3,2,1,0:T(8,128)(2,1)} copy(bf16[2,16,128,128]{3,2,1,0:T(8,128)(2,1)} %evoformer_pair.1) | data formatting | bytes 2097152

commit v5 on v4

--- a/solution.py
+++ b/solution.py
@@ -102,22 +102,42 @@
     def send_bias(m, g, live):
         for h in range(HEADS):
             bias_s[m, me, g, h] = jnp.where(live, bsc[:, h, :], MASKED).astype(jnp.bfloat16)
-        each_peer(lambda d: bias_copy(m, g, d).start())
-
-    def bias_copy(m, g, d):
+        bias_copy(m, g, 0, True).start()
+        each_chip(1, lambda e: bias_copy(m, g, e, False).start())
+
+    sibling = me + 1 - 2 * lax.rem(me, 2)
+
+    def bias_copy(m, g, e, relay):
+        block = lax.rem(me - 2 * e + count, count) if relay else me
+        peer = sibling if relay else lax.rem(me + 2 * e, count)
+        place = 2 * e + 1 if relay else 2 * e
         return pltpu.make_async_remote_copy(
-            src_ref=bias_s.at[m, me, g],
-            dst_ref=bias_s.at[m, me, g],
-            send_sem=bias_send.at[m, g, d],
-            recv_sem=bias_recv.at[m, g, d],
-            device_id=(grp, lax.rem(me + d, count)),
+            src_ref=bias_s.at[m, block, g],
+            dst_ref=bias_s.at[m, block, g],
+            send_sem=bias_send.at[m, g, place],
+            recv_sem=bias_recv.at[m, g, place],
+            device_id=(grp, peer),
             device_id_type=pl.DeviceIdType.MESH,
         )
+
+    def each_chip(first, act):
+        def one(e, carry):
+            act(e)
+            return carry
+
+        lax.fori_loop(first, count // 2, one, 0, unroll=count <= 8)
+
+    def relay_bias(m, g):
+        def one(e):
+            bias_copy(m, g, e, False).wait_recv()
+            bias_copy(m, g, e, True).start()
+
+        each_chip(1, one)
 
     def flip_copy(m, g, d, start, size):
         peer = lax.rem(me + d, count)
         return pltpu.make_async_remote_copy(
-            src_ref=send_s.at[g, pl.ds(start, size), peer],
+            src_ref=send_s.at[g, peer, pl.ds(start, size)],
             dst_ref=landed.at[m, g, pl.ds(first_row + start, size)],
             send_sem=flip_send.at[m, g, d],
             recv_sem=flip_recv.at[m, g, d],
@@ -126,11 +146,16 @@
         )
 
     def each_peer(act):
+        if count <= 8:
+            for d in sorted(range(1, count), key=lambda d: abs(2 * d - count)):
+                act(d)
+            return
+
         def one(d, carry):
             act(d)
             return carry
 
-        lax.fori_loop(1, count, one, 0, unroll=count <= 8)
+        lax.fori_loop(1, count, one, 0)
 
     def norm_bias(g):
         weights = head_weights(0)
@@ -237,8 +262,8 @@
                     done[rr] = (done[rr].astype(jnp.float32) + u).astype(jnp.bfloat16)
             for rr in range(RB):
                 r = b * RB + rr
-                send_s[g, r] = done[rr].reshape(count, R, C)
-                landed[m, g, first_row + r] = send_s[g, r, me]
+                send_s[g, :, r] = done[rr].reshape(count, R, C)
+                landed[m, g, first_row + r] = send_s[g, me, r]
             each_peer(lambda d: flip_copy(m, g, d, b * RB, RB).start())
             if m == 0:
                 first = done[0] if RB == 1 else jnp.concatenate(done, axis=0)
@@ -273,17 +298,19 @@
         return carry
 
     def start_node(g, carry):
+        relay_bias(0, g)
         project(0, g)
-        each_peer(lambda d: bias_copy(0, g, d).wait_recv())
+        each_chip(0, lambda e: bias_copy(0, g, e, True).wait_recv())
         turn_bias(g)
         attend(0, g, x_ref)
         send_bias(1, g, row < length_of(g))
         return carry
 
     def end_node(g, carry):
+        relay_bias(1, g)
         gather_flip(0, g, x1)
         project(1, g)
-        each_peer(lambda d: bias_copy(1, g, d).wait_recv())
+        each_chip(0, lambda e: bias_copy(1, g, e, True).wait_recv())
         each_peer(lambda d: flip_copy(0, g, d, 0, R).wait_send())
         attend(1, g, x1)
         return carry
@@ -292,7 +319,8 @@
         gather_flip(1, g, out_ref)
         each_peer(lambda d: flip_copy(1, g, d, 0, R).wait_send())
         for m in range(2):
-            each_peer(lambda d: bias_copy(m, g, d).wait_send())
+            each_chip(0, lambda e: bias_copy(m, g, e, True).wait_send())
+            each_chip(1, lambda e: bias_copy(m, g, e, False).wait_send())
         return carry
 
     for m in range(2):
@@ -331,7 +359,7 @@
             pltpu.VMEM((HEADS, W, W), bf),
             pltpu.VMEM((2, 3 * C, C), bf),
             pltpu.VMEM((2, count, G, HEADS, R, W), bf),
-            pltpu.VMEM((G, R, count, R, C), bf),
+            pltpu.VMEM((G, count, R, R, C), bf),
             pltpu.SemaphoreType.DMA((2, G, count)),
             pltpu.SemaphoreType.DMA((2, G, count)),
             pltpu.SemaphoreType.DMA((2, G, count)),

time: 70.8 us -> 68.1 us (0.962)
  Pallas kernels: 68.3 us -> 65.6 us
    pallas_call x1, Pallas kernels: 68.3 us -> 65.6 us  [on_device(): pl.pallas_call(partial(kernel, (count, G, R, W, C, RB)), out_shape=jax.Sh...]
where the time goes in v5:
time: 68.1 us; the launch traced here: 67.9 us
  Pallas kernels  65.6 us (96%)
  local copies, waits for them, and re-layouts  2.31 us (3%)
    pallas_call x1, Pallas kernels, on_device(): pl.pallas_call(partial(kernel, (count, G, R, W, C, RB)), out_shape=jax.Sh...  65.6 us
    unnamed x1, local copies, waits for them, and re-layouts  2.31 us

profile of v5, /device:TPU:0, one launch (start us, length us, event | category | flops | bytes accessed | tf_op | source)
XLA Modules:
  0.0 67.9 jit_solution(11640917715079840216)
XLA Ops:
  0.0 65.6 %evoformer_pair.1 = bf16[2,16,128,128]{3,2,1,0:T(8,128)(2,1)} custom-call(s32[8]{0:T(128)} %lens_ref.1, bf16[2,16,128,128]{3,2,1,0:T(8,128)(2,1)} %x_ref.1, f32[3,128]{1,0:T(4,128)} %gain_ref.1, f32[3,128]{1,0:T(4,128)} %shift_ref.1, bf16[2,128,512]{2,1,0:T(8,128)(2,1)} %proj_ref.1, bf16[2,4,128]{2,1,0:T(4,128)(2,1)} %bitcast.1, ...), custom_call_target="tpu_custom_call" | custom-call | tf_op jit(solution)/shard_map/evoformer_pair/pallas_call | solution.py:344
  65.6 2.3 %copy.11 = bf16[2,16,128,128]{3,2,1,0:T(8,128)(2,1)} copy(bf16[2,16,128,128]{3,2,1,0:T(8,128)(2,1)} %evoformer_pair.1) | data formatting | bytes 2097152

commit v6 on v5

--- a/solution.py
+++ b/solution.py
@@ -336,7 +336,7 @@
 ):
     G, R, W, C = pair_state.shape
     count = lax.axis_size("dap")
-    RB = 4 if W <= 128 else 1
+    RB = 2 if W <= 128 else 1
     wb = jnp.swapaxes(bias_proj, 1, 2)
     bf = jnp.bfloat16
     f32 = jnp.float32

time: 68.1 us -> 78.2 us (1.15)
  Pallas kernels: 65.6 us -> 75.7 us
    pallas_call x1, Pallas kernels: 65.6 us -> 75.7 us  [on_device(): pl.pallas_call(partial(kernel, (count, G, R, W, C, RB)), out_shape=jax.Sh...]
where the time goes in v6:
time: 78.2 us; the launch traced here: 78 us
  Pallas kernels  75.7 us (97%)
  local copies, waits for them, and re-layouts  2.31 us (3%)
    pallas_call x1, Pallas kernels, on_device(): pl.pallas_call(partial(kernel, (count, G, R, W, C, RB)), out_shape=jax.Sh...  75.7 us
    unnamed x1, local copies, waits for them, and re-layouts  2.31 us

profile of v6, /device:TPU:0, one launch (start us, length us, event | category | flops | bytes accessed | tf_op | source)
XLA Modules:
  0.0 78.0 jit_solution(6526925236287062933)
XLA Ops:
  0.0 75.7 %evoformer_pair.1 = bf16[2,16,128,128]{3,2,1,0:T(8,128)(2,1)} custom-call(s32[8]{0:T(128)} %lens_ref.1, bf16[2,16,128,128]{3,2,1,0:T(8,128)(2,1)} %x_ref.1, f32[3,128]{1,0:T(4,128)} %gain_ref.1, f32[3,128]{1,0:T(4,128)} %shift_ref.1, bf16[2,128,512]{2,1,0:T(8,128)(2,1)} %proj_ref.1, bf16[2,4,128]{2,1,0:T(4,128)(2,1)} %bitcast.1, ...), custom_call_target="tpu_custom_call" | custom-call | tf_op jit(solution)/shard_map/evoformer_pair/pallas_call | solution.py:344
  75.7 2.3 %copy.11 = bf16[2,16,128,128]{3,2,1,0:T(8,128)(2,1)} copy(bf16[2,16,128,128]{3,2,1,0:T(8,128)(2,1)} %evoformer_pair.1) | data formatting | bytes 2097152

commit v7 on v6

--- a/solution.py
+++ b/solution.py
@@ -336,7 +336,7 @@
 ):
     G, R, W, C = pair_state.shape
     count = lax.axis_size("dap")
-    RB = 2 if W <= 128 else 1
+    RB = 8 if W <= 128 else 1
     wb = jnp.swapaxes(bias_proj, 1, 2)
     bf = jnp.bfloat16
     f32 = jnp.float32

time: 78.2 us -> 67.8 us (0.87)
  Pallas kernels: 75.7 us -> 65.3 us
    pallas_call x1, Pallas kernels: 75.7 us -> 65.3 us  [on_device(): pl.pallas_call(partial(kernel, (count, G, R, W, C, RB)), out_shape=jax.Sh...]
where the time goes in v7:
time: 67.8 us; the launch traced here: 67.6 us
  Pallas kernels  65.3 us (96%)
  local copies, waits for them, and re-layouts  2.31 us (3%)
    pallas_call x1, Pallas kernels, on_device(): pl.pallas_call(partial(kernel, (count, G, R, W, C, RB)), out_shape=jax.Sh...  65.3 us
    unnamed x1, local copies, waits for them, and re-layouts  2.31 us

profile of v7, /device:TPU:0, one launch (start us, length us, event | category | flops | bytes accessed | tf_op | source)
XLA Modules:
  0.0 67.6 jit_solution(3720700993313093431)
XLA Ops:
  0.0 65.3 %evoformer_pair.1 = bf16[2,16,128,128]{3,2,1,0:T(8,128)(2,1)} custom-call(s32[8]{0:T(128)} %lens_ref.1, bf16[2,16,128,128]{3,2,1,0:T(8,128)(2,1)} %x_ref.1, f32[3,128]{1,0:T(4,128)} %gain_ref.1, f32[3,128]{1,0:T(4,128)} %shift_ref.1, bf16[2,128,512]{2,1,0:T(8,128)(2,1)} %proj_ref.1, bf16[2,4,128]{2,1,0:T(4,128)(2,1)} %bitcast.1, ...), custom_call_target="tpu_custom_call" | custom-call | tf_op jit(solution)/shard_map/evoformer_pair/pallas_call | solution.py:344
  65.3 2.3 %copy.11 = bf16[2,16,128,128]{3,2,1,0:T(8,128)(2,1)} copy(bf16[2,16,128,128]{3,2,1,0:T(8,128)(2,1)} %evoformer_pair.1) | data formatting | bytes 2097152
